TPU v7x, 256 devices: a whole 4x4x8 slice. The times are simulated.
256 devices in a mesh: vid: 16 (over y_hi, z), seq: 16 (over x, y_lo, core).
Axes of the slice: x: 4, y: 4 (y_hi: 2, y_lo: 2; y = y_hi * 2 + y_lo), z: 8, core: 2. Of those that a mesh axis runs over, the one named last changes fastest.
Arguments:
- video: bfloat16 [16, 512, 4096], P('vid', 'seq'), may hold values from -8 to 8
- video_length: int32 [16], P('vid'), may hold values from 128 to 512
- prompt: bfloat16 [16, 128, 4096], P('vid', 'seq'), may hold values from -6 to 6
- prompt_length: int32 [16], replicated, may hold values from 32 to 128
- prompt_choice: int32 [16], P('vid'), may hold values from 0 to 15
- ffn_gain: float32 [4096], replicated, may hold values from 0.1 to 1.9
- ffn_gate: bfloat16 [4096, 6144], P(None, 'seq'), may hold values from -0.09375 to 0.09375
- ffn_up: bfloat16 [4096, 6144], P(None, 'seq'), may hold values from -0.09375 to 0.09375
- ffn_down: bfloat16 [6144, 4096], P('seq'), may hold values from -0.078125 to 0.078125
- final_gain: float32 [4096], replicated, may hold values from 0.1 to 1.9
- video_gain: float32 [4096], replicated, may hold values from 0.1 to 1.9
- w_query: bfloat16 [4096, 4096], P('vid', 'seq'), may hold values from -1 to 1
- w_key: bfloat16 [4096, 4096], P('vid', 'seq'), may hold values from -3 to 3
- w_value: bfloat16 [4096, 4096], P('vid', 'seq'), may hold values from -0.09375 to 0.09375
- w_text_key: bfloat16 [4096, 4096], P('vid', 'seq'), may hold values from -0.09375 to 0.09375
- w_text_value: bfloat16 [4096, 4096], P('vid', 'seq'), may hold values from -0.09375 to 0.09375
- w_out: bfloat16 [4096, 4096], P('seq', 'vid'), may hold values from -0.09375 to 0.09375
Outputs:
- updated: bfloat16 [16, 512, 4096], P('vid', 'seq')
Inputs may be any that keep to these rules, and one draw needn't show every extreme that they name: `prompt_choice`: A prompt may serve several videos or none.
All inputs are finite; a program needn't handle non-finite values.
Results may differ from a plain program's by a relative error of at most 0.0085.
Values may be sent and summed in bfloat16 or wider, within the bound.
A program may use at most 128 MiB of HBM per device.

v0:
```python
import jax
import jax.numpy as jnp
from jax import lax
from jax.sharding import PartitionSpec as P

HD = 128


epsilon = 1e-06


def sent_to_all(x, axis):
    devices = lax.axis_size(axis)
    return lax.all_to_all(jnp.broadcast_to(x[None], (devices, *x.shape)), axis, 0, 0, tiled=True)


def laid_out(tiles, dim):
    lengths = list(tiles.shape[1:])
    lengths[dim] *= tiles.shape[0]
    return jnp.moveaxis(tiles, 0, dim).reshape(lengths)


def gathered_copies(x, axis, dim):
    tiles = sent_to_all(x, axis)
    return laid_out(tiles, dim)


def in_blocks(x, dim, devices):
    lengths = x.shape
    tiles = x.reshape(*lengths[:dim], devices, lengths[dim] // devices, *lengths[dim + 1 :])
    return jnp.moveaxis(tiles, dim, 0)


def sent_and_summed(x, axis, dim):
    tiles = in_blocks(x, dim, lax.axis_size(axis))
    arrived = lax.all_to_all(tiles, axis, split_axis=0, concat_axis=0, tiled=True)
    return arrived.astype(jnp.float32).sum(axis=0)


def side_by_side(arrays, axis, dim, along):
    both = jnp.concatenate(arrays, axis=along)
    whole, at, finished = (lax.all_gather(both, axis, axis=dim, tiled=True), 0, [])
    for a in arrays:
        finished.append(lax.slice_in_dim(whole, at, at + a.shape[along], axis=along))
        at += a.shape[along]
    return tuple(finished)


def rms_norm(values, gain):
    return values * lax.rsqrt(jnp.mean(values * values, axis=-1, keepdims=True) + epsilon) * gain


def prompt_path(
    prompt,
    prompt_length,
    prompt_choice,
    ffn_gain,
    ffn_gate,
    ffn_up,
    ffn_down,
    final_gain,
    w_text_key,
    w_text_value,
):
    gathered = gathered_copies(prompt, "seq", 1)[0]
    residual = gathered.astype(jnp.float32)
    ffn_normed = rms_norm(residual, ffn_gain).astype(jnp.bfloat16)
    gate_proj = jnp.dot(ffn_normed, ffn_gate, preferred_element_type=jnp.float32)
    up_proj = jnp.dot(ffn_normed, ffn_up, preferred_element_type=jnp.float32)
    ffn_hidden = (jax.nn.gelu(gate_proj, approximate=True) * up_proj).astype(jnp.bfloat16)
    partial_value = jnp.dot(ffn_hidden, ffn_down, preferred_element_type=jnp.float32)
    share = sent_and_summed(partial_value.astype(jnp.bfloat16), "seq", 0)
    own_rows = prompt[0].astype(jnp.float32)
    text_share = rms_norm(own_rows + share, final_gain).astype(jnp.bfloat16)
    text = gathered_copies(text_share, "seq", 0)
    blocks = side_by_side((w_text_key, w_text_value), "vid", 0, 1)
    key_sum = jnp.dot(text, blocks[0], preferred_element_type=jnp.float32)
    value_sum = jnp.dot(text, blocks[1], preferred_element_type=jnp.float32)
    text_key = key_sum.astype(jnp.bfloat16)[None]
    text_value = value_sum.astype(jnp.bfloat16)[None]
    wanted = prompt_choice[0]
    blocks = side_by_side((text_key, text_value), "vid", 0, 1)
    number = blocks[0].shape[0]
    chosen = jnp.arange(number, dtype=jnp.int32) == wanted
    picked_key = jnp.sum(
        jnp.where(chosen[:, None, None], blocks[0], jnp.zeros_like(blocks[0])), axis=0
    )
    picked_value = jnp.sum(
        jnp.where(chosen[:, None, None], blocks[1], jnp.zeros_like(blocks[1])), axis=0
    )
    prompt_ids = jnp.arange(prompt_length.shape[0], dtype=jnp.int32)
    text_live = jnp.sum(jnp.where(prompt_ids == wanted, prompt_length, 0))
    return (picked_key, picked_value, text_live)


def video_path(residual, video_gain, w_query, w_key, w_value):
    normed = rms_norm(residual, video_gain).astype(jnp.bfloat16)
    whole_rows = lax.all_gather(normed, "seq", axis=0, tiled=True)
    blocks = side_by_side((w_query, w_key, w_value), "vid", 0, 1)
    query_sum, key_sum, value_sum = tuple(
        (
            jnp.dot(whole_rows, blocks[index], preferred_element_type=jnp.float32)
            for index in range(3)
        )
    )
    return (
        query_sum.astype(jnp.bfloat16),
        key_sum.astype(jnp.bfloat16),
        value_sum.astype(jnp.bfloat16),
    )


def local(
    video,
    video_length,
    prompt,
    prompt_length,
    prompt_choice,
    ffn_gain,
    ffn_gate,
    ffn_up,
    ffn_down,
    final_gain,
    video_gain,
    w_query,
    w_key,
    w_value,
    w_text_key,
    w_text_value,
    w_out,
):
    residual = video[0].astype(jnp.float32)
    text_key, text_value, text_live = prompt_path(
        prompt,
        prompt_length,
        prompt_choice,
        ffn_gain,
        ffn_gate,
        ffn_up,
        ffn_down,
        final_gain,
        w_text_key,
        w_text_value,
    )
    query, key_rows, value_rows = video_path(residual, video_gain, w_query, w_key, w_value)
    out_full = gathered_copies(w_out, "vid", 1)
    total_rows = query.shape[0]
    text_rows = text_key.shape[0]
    width_here = query.shape[1]
    head_count = width_here // HD
    frame_length = video_length[0]
    joint_keys = jnp.concatenate([key_rows, text_key], axis=0).reshape(
        total_rows + text_rows, head_count, HD
    )
    joint_values = jnp.concatenate([value_rows, text_value], axis=0).reshape(
        total_rows + text_rows, head_count, HD
    )
    query_heads = query.reshape(total_rows, head_count, HD)
    scores = jnp.einsum(
        "qhd,khd->hqk", query_heads, joint_keys, preferred_element_type=jnp.float32
    ) * HD ** (-0.5)
    position = jnp.arange(total_rows + text_rows, dtype=jnp.int32)
    live_keys = jnp.where(
        position < total_rows, position < frame_length, position - total_rows < text_live
    )
    scores = jnp.where(live_keys[None, None, :], scores, -1e30)
    probs = jax.nn.softmax(scores, axis=-1).astype(jnp.bfloat16)
    attended = jnp.einsum("hqk,khd->qhd", probs, joint_values, preferred_element_type=jnp.float32)
    attended = attended.astype(jnp.bfloat16).reshape(total_rows, width_here)
    local_rows = video.shape[1]
    projected = lax.psum_scatter(
        jnp.dot(attended, out_full, preferred_element_type=jnp.float32).astype(jnp.bfloat16),
        "seq",
        scatter_dimension=0,
        tiled=True,
    ).astype(jnp.float32)
    row_position = lax.axis_index("seq") * local_rows + jnp.arange(local_rows, dtype=jnp.int32)
    row_live = row_position < frame_length
    updated = residual + jnp.where(row_live[:, None], projected, 0.0)
    return updated.astype(jnp.bfloat16)[None]


def solution(mesh):
    in_specs = (
        P("vid", "seq", None),
        P("vid"),
        P("vid", "seq", None),
        P(),
        P("vid"),
        P(),
        P(None, "seq"),
        P(None, "seq"),
        P("seq", None),
        P(),
        P(),
        P("vid", "seq"),
        P("vid", "seq"),
        P("vid", "seq"),
        P("vid", "seq"),
        P("vid", "seq"),
        P("seq", "vid"),
    )
    out_specs = P("vid", "seq", None)
    return jax.shard_map(local, mesh=mesh, in_specs=in_specs, out_specs=out_specs, check_vma=False)
```

profile of v0, /device:TPU:1, one launch (start us, length us, event | category | flops | bytes accessed | tf_op | source)
XLA Modules:
  0.0 482.7 jit_solution(16630161298644301142)
XLA Ops:
  6.5 0.0 copy-start
  6.5 0.0 all-gather.9.cloned.1.call-start
  6.5 1.8 pad_maximum_fusion.2
  8.4 0.0 all-gather.9.cloned.1.call-update
  8.4 0.0 all-gather.11.cloned.1.call-start
  8.5 0.9 broadcast_in_dim.85
  9.4 22.0 %all_to_all.20 = bf16[16,1,8,4096]{3,2,1,0:T(8,128)(2,1)S(1)} all-to-all(bf16[16,1,8,4096]{3,2,1,0:T(8,128)(2,1)S(1)} %broadcast_in_dim.85), channel_id=1, replica_groups=mesh['vid'=16,'seq'=16] {'seq'}, dimensions={0} | all-to-all | bytes 2097152 | tf_op jit(solution)/shard_map/all_to_all | solution.py:14
  31.4 1.0 copy-done.1
  32.3 0.3 fusion.5
  32.6 0.1 rsqrt.29
  32.7 0.0 copy-done.6
  32.7 3.0 fusion.70
  35.8 0.0 copy-done
  35.8 4.7 fusion.1
  40.5 20.1 %all_to_all.21 = bf16[16,8,4096]{2,1,0:T(8,128)(2,1)S(1)} all-to-all(bf16[16,8,4096]{2,1,0:T(8,128)(2,1)} %fusion.1), channel_id=1, replica_groups=mesh['vid'=16,'seq'=16] {'seq'}, dimensions={0} | all-to-all | bytes 2097152 | tf_op jit(solution)/shard_map/all_to_all | solution.py:36
  60.6 0.1 convert_reduce_fusion
  60.7 0.0 copy-done.4
  60.7 0.1 multiply_reduce_fusion
  60.9 0.0 copy-done.7
  60.9 0.1 fusion.76
  61.0 0.1 broadcast_in_dim.87
  61.1 21.4 %all_to_all.22 = bf16[16,8,4096]{2,1,0:T(8,128)(2,1)} all-to-all(bf16[16,8,4096]{2,1,0:T(8,128)(2,1)S(1)} %broadcast_in_dim.87), channel_id=1, replica_groups=mesh['vid'=16,'seq'=16] {'seq'}, dimensions={0} | all-to-all | bytes 2097152 | tf_op jit(solution)/shard_map/all_to_all | solution.py:14
  82.4 41.5 %all-gather.9.cloned.1.call-done = bf16[4096,512]{1,0:T(8,128)(2,1)} async-done(((bf16[256,512]{1,0:T(8,128)(2,1)}), bf16[4096,512]{1,0:T(8,128)(2,1)}) %all-gather.9.cloned.1.call-update) | async-done | bytes 4194320 | tf_op jit(solution)/shard_map/all_gather | solution.py:42
  123.9 2.4 fusion.38
  126.4 0.0 copy-done.3
  126.4 0.0 copy-start.2
  126.4 0.0 copy-start.8
  126.4 0.0 copy-start.5
  126.4 2.1 fusion.41
  128.5 0.7 pad_maximum_fusion.3
  129.2 0.0 all-gather.11.cloned.1.call-update
  129.2 0.0 all-gather.5.cloned.1.call-start
  129.2 0.0 copy-done.2
  129.2 0.2 fusion.48
  129.4 0.0 copy-done.8
  129.4 0.8 fusion.50
  130.3 0.0 all-gather.5.cloned.1.call-update
  130.3 0.0 all-gather.7.cloned.1.call-start
  130.3 1.7 pad_maximum_fusion
  132.1 0.0 all-gather.7.cloned.1.call-update
  132.1 1.0 copy.32
  133.1 1.6 broadcast_in_dim.93
  134.7 4.6 all-to-all-start.3
  139.3 0.2 reduce-scatter.2.cloned.1.call-start
  140.8 0.0 copy-done.10
  140.8 0.7 select_reduce_fusion
  141.5 0.7 fusion.81
  142.2 82.2 %all-gather.11.cloned.1.call-done = bf16[16,256,256]{2,1,0:T(8,128)(2,1)} async-done(((bf16[1,256,256]{2,1,0:T(8,128)(2,1)}), bf16[16,256,256]{2,1,0:T(8,128)(2,1)}) %all-gather.11.cloned.1.call-update) | async-done | bytes 2097168 | tf_op jit(solution)/shard_map/all_gather | solution.py:42
  224.4 1.9 fusion.44
  226.4 40.4 %all-gather.5.cloned.1.call-done = bf16[512,4096]{1,0:T(8,128)(2,1)} async-done(((bf16[32,4096]{1,0:T(8,128)(2,1)}), bf16[512,4096]{1,0:T(8,128)(2,1)}) %all-gather.5.cloned.1.call-update) | async-done | bytes 4194320 | tf_op jit(solution)/shard_map/all_gather | solution.py:98
  266.8 117.1 %all-gather.7.cloned.1.call-done = bf16[4096,768]{1,0:T(8,128)(2,1)} async-done(((bf16[256,768]{1,0:T(8,128)(2,1)}), bf16[4096,768]{1,0:T(8,128)(2,1)}) %all-gather.7.cloned.1.call-update) | async-done | bytes 6291472 | tf_op jit(solution)/shard_map/all_gather | solution.py:42
  383.9 4.1 fusion.22
  388.0 0.7 pad_maximum_fusion.1
  388.7 1.9 copy.34
  390.6 5.0 %fusion.25 = bf16[512,256]{0,1:T(8,128)(2,1)} fusion(bf16[512,4096]{1,0:T(8,128)(2,1)} %all-gather.5.cloned.1.call-done, bf16[4096,768]{1,0:T(8,128)(2,1)} %all-gather.7.cloned.1.call-done), kind=kOutput, calls=%fused_computation.31 | convolution fusion | flops 1073872896 | bytes 6553600 | tf_op jit(solution)/shard_map/dot_general | solution.py:102
  395.6 0.0 copy-done.9
  395.6 3.6 fusion.28
  399.2 2.2 fusion.91
  401.4 3.2 fusion.21
  404.5 0.0 all-to-all-done.3
  404.6 4.9 %convolution_convert_fusion = bf16[512,4096]{1,0:T(8,128)(2,1)} fusion(bf16[512,256]{0,1:T(8,128)(2,1)} %bitcast.94, bf16[256,4096]{0,1:T(8,128)(2,1)} %bitcast.17), kind=kOutput, calls=%fused_computation.1 | convolution fusion | flops 1075838976 | bytes 6553600 | tf_op jit(solution)/shard_map/dot_general | solution.py:172
  409.5 0.0 reduce-scatter.2.cloned.1.call-update
  409.5 64.8 %reduce-scatter.2.cloned.1.call-done = bf16[32,4096]{1,0:T(8,128)(2,1)} async-done(((bf16[512,4096]{1,0:T(8,128)(2,1)}), bf16[32,4096]{1,0:T(8,128)(2,1)}) %reduce-scatter.2.cloned.1.call-update) | async-done | bytes 262160 | tf_op jit(solution)/shard_map/reduce_scatter | solution.py:171
  474.4 1.8 fusion.59
  (13 shorter events, 0.1 us)
Async XLA Ops:
  6.5 29.2 %copy-start = (bf16[384,4096]{1,0:T(8,128)(2,1)S(1)}, bf16[384,4096]{1,0:T(8,128)(2,1)}, u32[]{:S(2)}) copy-start(bf16[384,4096]{1,0:T(8,128)(2,1)} %param.25) | copy-start | bytes 9437188
  6.5 26.2 %copy-start.6 = (f32[4096]{0:T(1024)S(1)}, f32[4096]{0:T(1024)}, u32[]{:S(2)}) copy-start(f32[4096]{0:T(1024)} %param.22) | copy-start | bytes 49156
  6.5 117.4 %all-gather.9.cloned.1.call-start = ((), (), s32[]{:S(2)}) async-start(), calls=%async_computation.7 | async-start | bytes 4456448 | tf_op jit(solution)/shard_map/all_gather | solution.py:42
  8.4 216.0 %all-gather.11.cloned.1.call-start = ((), (), s32[]{:S(2)}) async-start(), calls=%async_computation.8 | async-start | bytes 2228224 | tf_op jit(solution)/shard_map/all_gather | solution.py:42
  31.4 1.0 copy-start.1
  40.5 20.2 %copy-start.4 = (bf16[1,8,4096]{2,1,0:T(8,128)(2,1)S(1)}, bf16[1,8,4096]{2,1,0:T(8,128)(2,1)}, u32[]{:S(2)}) copy-start(bf16[1,8,4096]{2,1,0:T(8,128)(2,1)} %param.19) | copy-start | bytes 196612
  40.5 20.4 %copy-start.7 = (f32[4096]{0:T(1024)S(1)}, f32[4096]{0:T(1024)}, u32[]{:S(2)}) copy-start(f32[4096]{0:T(1024)} %param.26) | copy-start | bytes 49156
  123.9 2.4 copy-start.3
  126.4 2.9 copy-start.2
  126.4 3.0 copy-start.8
  126.4 3.9 copy-start.5
  129.2 137.6 %all-gather.5.cloned.1.call-start = ((), (), s32[]{:S(2)}) async-start(), calls=%async_computation.5 | async-start | bytes 4456448 | tf_op jit(solution)/shard_map/all_gather | solution.py:98
  130.3 253.6 %all-gather.7.cloned.1.call-start = ((), (), s32[]{:S(2)}) async-start(), calls=%async_computation.6 | async-start | bytes 6684672 | tf_op jit(solution)/shard_map/all_gather | solution.py:42
  134.7 6.1 %copy-start.10 = (s32[16]{0:T(128)S(1)}, s32[16]{0:T(128)}, u32[]{:S(2)}) copy-start(s32[16]{0:T(128)} %param.20) | copy-start | bytes 196
  134.7 269.9 %all-to-all-start.3 = ((bf16[16,256,256]{1,2,0:T(8,128)(2,1)}), bf16[16,256,256]{1,2,0:T(8,128)(2,1)}, u32[]{:S(2)}, u32[]{:S(2)}) async-start(bf16[16,256,256]{1,2,0:T(8,128)(2,1)} %broadcast_in_dim.93), calls=%async_computation.3 | async-start | bytes 4194304 | tf_op jit(solution)/shard_map/all_to_all | solution.py:14
  139.3 335.1 %reduce-scatter.2.cloned.1.call-start = ((), (), s32[]{:S(2)}) async-start(), calls=%async_computation.9 | async-start | bytes 4456448 | tf_op jit(solution)/shard_map/reduce_scatter | solution.py:171
  390.6 5.0 %copy-start.9 = (bf16[512,4096]{1,0:T(8,128)(2,1)S(1)}, bf16[512,4096]{1,0:T(8,128)(2,1)}, u32[]{:S(2)}) copy-start(bf16[512,4096]{1,0:T(8,128)(2,1)} %all-gather.5.cloned.1.call-done) | copy-start | bytes 12582916
Sparse Core Ops, SparseCore 0:
  9.9 113.9 all-gather.8
  129.3 95.0 all-gather.10
  226.3 40.4 all-gather.4
  269.3 114.5 all-gather.6
  409.6 64.6 reduce-scatter.1
where the time goes:
time: 485 us; the launch traced here: 483 us
  waiting for transfers between devices  346 us (71%)
  blocking collectives  63.4 us (13%)
  matrix products  35.2 us (7%)
  between operations  14.6 us (3%)
  other arithmetic  11.8 us (2%)
  local copies, waits for them, and re-layouts  6.59 us (1%)
  starting transfers between devices  4.91 us (1%)
    all_gather x3, waiting for transfers between devices, side_by_side(): lax.all_gather(both, axis, axis=dim, tiled=True)  241 us
    reduce_scatter x1, waiting for transfers between devices, local(): lax.psum_scatter(jnp.dot(attended, out_full, preferred_element_type=jnp.f...  64.8 us
    all_to_all x2, blocking collectives, sent_to_all(): lax.all_to_all(jnp.broadcast_to(x[None], (devices, *x.shape)), axis, 0, 0...  43.3 us
    all_gather x1, waiting for transfers between devices, video_path(): whole_rows = lax.all_gather(normed, 'seq', axis=0, tiled=True)  40.4 us
    all_to_all x1, blocking collectives, sent_and_summed(): lax.all_to_all(tiles, axis, split_axis=0, concat_axis=0, tiled=True)  20.1 us
    dot_general x3, matrix products, video_path(): jnp.dot(whole_rows, blocks[index], preferred_element_type=jnp.float32)  12.7 us
  transfers between devices with their start and end apart: 6, of which 5 were waited for; matrix products, arithmetic and copies ran while one was open for 8% of the time, Pallas kernels for 0%

commit v1 on v0

v1 whole, which is shorter than its diff:
```python
import jax
import jax.numpy as jnp
from jax import lax
from jax.experimental import pallas as pl
from jax.experimental.pallas import tpu as pltpu
from jax.sharding import PartitionSpec as P

HD = 128
EPSILON = 1e-06
MESH = pl.DeviceIdType.MESH
BF = jnp.bfloat16
F32 = jnp.float32

TK, TV, Q, K, V, O, PROMPT = range(7)


def rms_norm(values, gain):
    return values * lax.rsqrt(jnp.mean(values * values, axis=-1, keepdims=True) + EPSILON) * gain


def kernel(
    length_ref,
    prompt_length_ref,
    choice_ref,
    video_ref,
    prompt_ref,
    ffn_gain_ref,
    final_gain_ref,
    video_gain_ref,
    gate_hbm,
    up_hbm,
    down_hbm,
    w_text_key,
    w_text_value,
    w_query,
    w_key,
    w_value,
    w_out,
    out_ref,
    W,
    PB,
    SEL,
    PG,
    FN,
    gate_ref,
    up_ref,
    down_ref,
    gate_acc,
    up_acc,
    hidden,
    FP,
    FR,
    TX,
    TG,
    NV,
    XG,
    q_acc,
    k_acc,
    v_acc,
    queries,
    keys,
    values,
    SB,
    RR,
    info_own,
    info,
    ffn_sem,
    ring_recv,
    ring_send,
    swap_send,
    sib_recv,
    info_sem,
    group_recv,
    group_send,
    group_send0,
):
    vid, seq = lax.axis_index("vid"), lax.axis_index("seq")
    yh, z = vid // 8, vid % 8
    x, yl, c = seq // 4, (seq // 2) % 2, seq % 2
    y = yh * 2 + yl
    diag = c == yh
    head_block = x * 4 + yl * 2 + yh

    partner = ((1 - yh) * 8 + z, seq + 1 - 2 * c)
    sibling = (vid, seq + 1 - 2 * c)
    z_right = (yh * 8 + (z + 1) % 8, seq)
    z_left = (yh * 8 + (z + 7) % 8, seq)

    def to_chip(k):
        xk, yk = (x + k // 4) % 4, (y + k % 4) % 4
        return ((yk // 2) * 8 + z, xk * 4 + (yk % 2) * 2 + yh)

    def place(k):
        return ((x + k // 4) % 4) * 4 + ((yl + (k // 2) % 2) % 2) * 2 + (c + k % 2) % 2

    def local(src, dst, sem):
        return pltpu.make_async_copy(src, dst, sem)

    def remote(src, dst, send, recv, device):
        return pltpu.make_async_remote_copy(
            src_ref=src, dst_ref=dst, send_sem=send, recv_sem=recv, device_id=device, device_id_type=MESH
        )

    ffn_copies = [
        local(gate_hbm, gate_ref, ffn_sem.at[0]),
        local(up_hbm, up_ref, ffn_sem.at[1]),
        local(down_hbm, down_ref, ffn_sem.at[2]),
    ]
    for copy in ffn_copies:
        copy.start()

    barrier = pltpu.get_barrier_semaphore()

    def greet(k, carry):
        seq_k = (seq + k) % 16
        vid_k = ((yh + k // 16) % 2) * 8 + z
        pl.semaphore_signal(barrier, inc=1, device_id=(vid_k, seq_k), device_id_type=MESH)
        return carry

    lax.fori_loop(1, 32, greet, 0)
    for neighbour in (z_left, z_right):
        pl.semaphore_signal(barrier, inc=1, device_id=neighbour, device_id_type=MESH)

    choice = choice_ref[0]
    row = lax.broadcasted_iota(jnp.int32, (8, 128), 0)
    text_live = prompt_length_ref[choice]
    info_own[...] = jnp.where(row == 0, choice, jnp.where(row == 1, length_ref[0], text_live))

    pl.semaphore_wait(barrier, 33)

    sources = [w_text_key, w_text_value, w_query, w_key, w_value, w_out, prompt_ref.at[0]]

    def slot(w, block):
        return PB.at[block] if w == PROMPT else W.at[w, block]

    def swap_copy(w):
        return remote(
            sources[w], slot(w, (1 - c) * 8 + z), swap_send.at[w], ring_recv.at[w, z], partner
        )

    def swap_local(w):
        return local(sources[w], slot(w, c * 8 + z), ring_recv.at[w, z])

    info_copy = remote(info_own, info, swap_send.at[7], info_sem, partner)
    info_local = local(info_own, info, info_sem)

    @pl.when(diag)
    def _():
        swap_local(PROMPT).start()
        info_local.start()
        for w in range(6):
            swap_local(w).start()

    @pl.when(jnp.logical_not(diag))
    def _():
        swap_copy(PROMPT).start()
        info_copy.start()
        for w in range(6):
            swap_copy(w).start()

    def ring_wait(w, zz):
        ref = slot(w, c * 8 + zz)
        local(ref, ref, ring_recv.at[w, zz]).wait()

    def ring_to(w, zz, device):
        ref = slot(w, c * 8 + zz)
        remote(ref, ref, ring_send.at[w], ring_recv.at[w, zz], device).start()

    def to_sibling(w, zz):
        ref = slot(w, c * 8 + zz)
        remote(ref, ref, ring_send.at[w], sib_recv.at[w], sibling).start()

    def own(w):
        ring_wait(w, z)
        ring_to(w, z, z_right)
        ring_to(w, z, z_left)
        to_sibling(w, z)

    def hop(w, k):
        right_hops = 4 if w % 2 == 0 else 3
        left_hops = 7 - right_hops
        from_left, from_right = (z + 8 - k) % 8, (z + k) % 8
        if k <= right_hops:
            ring_wait(w, from_left)
            if k < right_hops:
                ring_to(w, from_left, z_right)
        if k <= left_hops:
            ring_wait(w, from_right)
            if k < left_hops:
                ring_to(w, from_right, z_left)
        if k <= right_hops:
            to_sibling(w, from_left)
        if k <= left_hops:
            to_sibling(w, from_right)

    def sibling_wait(w):
        ref = PB.at[pl.ds(0, 8)] if w == PROMPT else W.at[w, pl.ds(0, 8)]
        local(ref, ref, sib_recv.at[w]).wait()

    own(PROMPT)
    own(TK)
    own(TV)

    NV[...] = rms_norm(video_ref[0].astype(F32), video_gain_ref[...]).astype(BF)

    for k in range(1, 5):
        hop(PROMPT, k)
    hop(TK, 1)
    hop(TV, 1)

    sibling_wait(PROMPT)
    local(info, info, info_sem).wait()
    wanted = info[0:1, 0:1]

    def pick(i, total):
        return total + jnp.where(wanted == i, PB[i].astype(F32), 0.0)

    SEL[...] = lax.fori_loop(0, 16, pick, jnp.zeros(SEL.shape, F32)).astype(BF)

    PROMPTS, SUMS, TEXT, VIDEO, OUT = range(5)

    def send_prompt(k):
        return remote(
            SEL, PG.at[head_block], group_send.at[PROMPTS], group_recv.at[PROMPTS], (c * 8 + z, place(k))
        )

    def spread(first, last, make):
        def step(k, carry):
            make(k).start()
            return carry

        lax.fori_loop(first, last, step, 0)

    def first_send(copy, copy_local, group):
        @pl.when(diag)
        def _():
            copy_local.start()

        @pl.when(jnp.logical_not(diag))
        def _():
            copy.start()

    prompt0 = remote(
        SEL, PG.at[head_block], group_send0.at[PROMPTS], group_recv.at[PROMPTS], (c * 8 + z, seq)
    )
    first_send(prompt0, local(SEL, PG.at[head_block], group_recv.at[PROMPTS]), PROMPTS)
    spread(1, 16, send_prompt)

    def send_video(k):
        return remote(NV, XG.at[seq], group_send.at[VIDEO], group_recv.at[VIDEO], to_chip(k))

    video0 = remote(NV, XG.at[seq], group_send0.at[VIDEO], group_recv.at[VIDEO], to_chip(0))
    first_send(video0, local(NV, XG.at[seq], group_recv.at[VIDEO]), VIDEO)
    spread(1, 16, send_video)

    hop(TK, 2)
    hop(TV, 2)
    own(Q)
    own(K)

    local(PG, PG, group_recv.at[PROMPTS]).wait()

    def norm_rows(i, carry):
        rows = PG[pl.ds(2 * i, 2)].astype(F32).reshape(16, PG.shape[2])
        FN[pl.ds(pl.multiple_of(i * 16, 16), 16), :] = rms_norm(rows, ffn_gain_ref[...]).astype(BF)
        return carry

    lax.fori_loop(0, 8, norm_rows, 0)
    ffn_copies[0].wait()
    ffn_copies[1].wait()
    gate_acc[...] = jnp.zeros_like(gate_acc)
    up_acc[...] = jnp.zeros_like(up_acc)

    def gate_up(i, carry):
        at = pl.ds(pl.multiple_of(i * 512, 512), 512)
        rows = FN[:, at]
        gate_acc[...] += jnp.dot(rows, gate_ref[at, :], preferred_element_type=F32)
        up_acc[...] += jnp.dot(rows, up_ref[at, :], preferred_element_type=F32)
        return carry

    lax.fori_loop(0, 8, gate_up, 0)
    hidden[...] = (jax.nn.gelu(gate_acc[...], approximate=True) * up_acc[...]).astype(BF)

    hop(TK, 3)
    hop(TV, 3)
    hop(Q, 1)
    hop(K, 1)
    ffn_copies[2].wait()

    def down_proj(i, carry):
        at = pl.ds(pl.multiple_of(i * 256, 256), 256)
        part = jnp.dot(hidden[...], down_ref[:, at], preferred_element_type=F32)
        FP[:, :, at] = part.reshape(16, 8, 256).astype(BF)
        return carry

    lax.fori_loop(0, 16, down_proj, 0)

    def send_sums(k):
        return remote(
            FP.at[place(k)], FR.at[seq], group_send.at[SUMS], group_recv.at[SUMS], (vid, place(k))
        )

    local(FP.at[seq], FR.at[seq], group_recv.at[SUMS]).start()
    spread(1, 16, send_sums)

    hop(TK, 4)
    hop(TV, 4)
    hop(Q, 2)
    hop(K, 2)
    own(V)
    own(O)

    local(FR, FR, group_recv.at[SUMS]).wait()
    encoded = lax.fori_loop(
        0, 16, lambda i, total: total + FR[i].astype(F32), jnp.zeros(TX.shape, F32)
    )
    encoded = PG[seq].astype(F32) + encoded
    TX[...] = rms_norm(encoded, final_gain_ref[...]).astype(BF)

    def send_text(k):
        return remote(TX, TG.at[seq], group_send.at[TEXT], group_recv.at[TEXT], to_chip(k))

    text0 = remote(TX, TG.at[seq], group_send0.at[TEXT], group_recv.at[TEXT], to_chip(0))
    first_send(text0, local(TX, TG.at[seq], group_recv.at[TEXT]), TEXT)
    spread(1, 16, send_text)

    hop(Q, 3)
    hop(K, 3)
    hop(V, 1)
    hop(O, 1)
    hop(Q, 4)
    hop(K, 4)
    hop(V, 2)
    hop(O, 2)

    local(XG, XG, group_recv.at[VIDEO]).wait()
    sibling_wait(Q)
    sibling_wait(K)
    q_acc[...] = jnp.zeros_like(q_acc)
    k_acc[...] = jnp.zeros_like(k_acc)

    def video_rows(j):
        at = pl.ds(pl.multiple_of(j * 256, 256), 256)
        return XG[:, :, at].reshape(512, 256)

    def query_key(j, carry):
        rows = video_rows(j)
        q_acc[...] += jnp.dot(rows, W[Q, j], preferred_element_type=F32)
        k_acc[...] += jnp.dot(rows, W[K, j], preferred_element_type=F32)
        return carry

    lax.fori_loop(0, 16, query_key, 0)
    queries[...] = q_acc[...].astype(BF)
    keys[pl.ds(0, 512), :] = k_acc[...].astype(BF)

    hop(V, 3)
    hop(O, 3)

    local(TG, TG, group_recv.at[TEXT]).wait()
    sibling_wait(TK)
    sibling_wait(TV)

    def text_key_value(j, carry):
        at = pl.ds(pl.multiple_of(j * 256, 256), 256)
        rows = TG[:, :, at].astype(F32).reshape(128, 256).astype(BF)
        key_sum, value_sum = carry
        key_sum = key_sum + jnp.dot(rows, W[TK, j], preferred_element_type=F32)
        value_sum = value_sum + jnp.dot(rows, W[TV, j], preferred_element_type=F32)
        return key_sum, value_sum

    zero = jnp.zeros((128, 256), F32)
    text_key, text_value = lax.fori_loop(0, 16, text_key_value, (zero, zero))
    keys[pl.ds(512, 128), :] = text_key.astype(BF)
    values[pl.ds(512, 128), :] = text_value.astype(BF)

    hop(V, 4)
    hop(O, 4)
    sibling_wait(V)
    v_acc[...] = jnp.zeros_like(v_acc)

    def value_rows(j, carry):
        v_acc[...] += jnp.dot(video_rows(j), W[V, j], preferred_element_type=F32)
        return carry

    lax.fori_loop(0, 16, value_rows, 0)
    values[pl.ds(0, 512), :] = v_acc[...].astype(BF)
    sibling_wait(O)

    position = lax.broadcasted_iota(jnp.int32, (1, 640), 1)
    live = position < jnp.where(position < 512, info[1:2, 0:1], info[2:3, 0:1] + 512)

    def send_out(block):
        return remote(
            SB.at[block], RR.at[head_block], group_send.at[OUT], group_recv.at[OUT], (c * 8 + z, block)
        )

    out0_local = local(SB.at[seq], RR.at[head_block], group_recv.at[OUT])
    out0 = remote(
        SB.at[seq], RR.at[head_block], group_send0.at[OUT], group_recv.at[OUT], (c * 8 + z, seq)
    )

    def attend(i, carry):
        part = (x + i) % 4
        rows = pl.ds(pl.multiple_of(part * 128, 128), 128)
        heads = []
        for h in range(2):
            lanes = pl.ds(h * HD, HD)
            scores = lax.dot_general(
                queries[rows, lanes], keys[:, lanes], (((1,), (1,)), ((), ())), preferred_element_type=F32
            )
            scores = jnp.where(live, scores * HD ** (-0.5), -1e30)
            e = jnp.exp(scores - jnp.max(scores, axis=-1, keepdims=True))
            probs = (e / jnp.sum(e, axis=-1, keepdims=True)).astype(BF)
            heads.append(jnp.dot(probs, values[:, lanes], preferred_element_type=F32).astype(BF))
        attended = jnp.concatenate(heads, axis=1)

        for j in range(16):
            projected = jnp.dot(attended, W[O, j], preferred_element_type=F32)
            SB[pl.ds(part * 4, 4), :, pl.ds(j * 256, 256)] = projected.reshape(4, 32, 256).astype(BF)

        def send(k, carry):
            block = part * 4 + (seq + k) % 4

            @pl.when(block != seq)
            def _():
                send_out(block).start()

            @pl.when(block == seq)
            def _():
                first_send(out0, out0_local, OUT)

            return carry

        lax.fori_loop(0, 4, send, 0)
        return carry

    lax.fori_loop(0, 4, attend, 0)

    local(RR, RR, group_recv.at[OUT]).wait()
    row_position = seq * 32 + lax.broadcasted_iota(jnp.int32, (32, 1), 0)
    row_live = row_position < length_ref[0]

    def add_up(j, carry):
        at = pl.ds(pl.multiple_of(j * 512, 512), 512)
        total = RR[0, :, at].astype(F32)
        for i in range(1, 16):
            total = total + RR[i, :, at].astype(F32)
        updated = video_ref[0, :, at].astype(F32) + jnp.where(row_live, total, 0.0)
        out_ref[0, :, at] = updated.astype(BF)
        return carry

    lax.fori_loop(0, 8, add_up, 0)

    @pl.when(jnp.logical_not(diag))
    def _():
        for w in range(7):
            swap_copy(w).wait_send()
        info_copy.wait_send()
        for group, copy in ((PROMPTS, prompt0), (TEXT, text0), (VIDEO, video0), (OUT, out0)):
            copy.wait_send()

    for w in range(7):
        ref = PB.at[pl.ds(0, 15)] if w == PROMPT else W.at[w, pl.ds(0, 15)]
        local(ref, ref, ring_send.at[w]).wait()
    for group, buffer in ((PROMPTS, PG), (SUMS, FR), (TEXT, TG), (VIDEO, XG), (OUT, RR)):
        ref = buffer.at[pl.ds(0, 15)]
        local(ref, ref, group_send.at[group]).wait()


def block(
    video,
    video_length,
    prompt,
    prompt_length,
    prompt_choice,
    ffn_gain,
    ffn_gate,
    ffn_up,
    ffn_down,
    final_gain,
    video_gain,
    w_query,
    w_key,
    w_value,
    w_text_key,
    w_text_value,
    w_out,
):
    smem = pl.BlockSpec(memory_space=pltpu.SMEM)
    vmem = pl.BlockSpec(memory_space=pltpu.VMEM)
    hbm = pl.BlockSpec(memory_space=pl.ANY)
    dma = pltpu.SemaphoreType.DMA
    width = 4096
    return pl.pallas_call(
        kernel,
        out_shape=jax.ShapeDtypeStruct(video.shape, video.dtype),
        in_specs=[smem] * 3 + [vmem] * 5 + [hbm] * 9,
        out_specs=vmem,
        scratch_shapes=[
            pltpu.VMEM((6, 16, 256, 256), BF),
            pltpu.VMEM((16, 8, width), BF),
            pltpu.VMEM((8, width), BF),
            pltpu.VMEM((16, 8, width), BF),
            pltpu.VMEM((128, width), BF),
            pltpu.VMEM(ffn_gate.shape, BF),
            pltpu.VMEM(ffn_up.shape, BF),
            pltpu.VMEM(ffn_down.shape, BF),
            pltpu.VMEM((128, 384), F32),
            pltpu.VMEM((128, 384), F32),
            pltpu.VMEM((128, 384), BF),
            pltpu.VMEM((16, 8, width), BF),
            pltpu.VMEM((16, 8, width), BF),
            pltpu.VMEM((8, width), BF),
            pltpu.VMEM((16, 8, width), BF),
            pltpu.VMEM((32, width), BF),
            pltpu.VMEM((16, 32, width), BF),
            pltpu.VMEM((512, 256), F32),
            pltpu.VMEM((512, 256), F32),
            pltpu.VMEM((512, 256), F32),
            pltpu.VMEM((512, 256), BF),
            pltpu.VMEM((640, 256), BF),
            pltpu.VMEM((640, 256), BF),
            pltpu.VMEM((16, 32, width), BF),
            pltpu.VMEM((16, 32, width), BF),
            pltpu.VMEM((8, 128), jnp.int32),
            pltpu.VMEM((8, 128), jnp.int32),
            dma((3,)),
            dma((7, 8)),
            dma((7,)),
            dma((8,)),
            dma((7,)),
            dma,
            dma((5,)),
            dma((5,)),
            dma((5,)),
        ],
        compiler_params=pltpu.CompilerParams(
            collective_id=0, has_side_effects=True, vmem_limit_bytes=58 * 1024 * 1024
        ),
        name="joint_attention",
    )(
        video_length,
        prompt_length,
        prompt_choice,
        video,
        prompt,
        ffn_gain.reshape(1, -1),
        final_gain.reshape(1, -1),
        video_gain.reshape(1, -1),
        ffn_gate,
        ffn_up,
        ffn_down,
        w_text_key,
        w_text_value,
        w_query,
        w_key,
        w_value,
        w_out,
    )


def solution(mesh):
    in_specs = (
        P("vid", "seq", None),
        P("vid"),
        P("vid", "seq", None),
        P(),
        P("vid"),
        P(),
        P(None, "seq"),
        P(None, "seq"),
        P("seq", None),
        P(),
        P(),
        P("vid", "seq"),
        P("vid", "seq"),
        P("vid", "seq"),
        P("vid", "seq"),
        P("vid", "seq"),
        P("seq", "vid"),
    )
    out_specs = P("vid", "seq", None)
    return jax.shard_map(block, mesh=mesh, in_specs=in_specs, out_specs=out_specs, check_vma=False)
```

time: 485 us -> 219 us (0.45)
  waiting for transfers between devices: 346 us -> 0 us
  Pallas kernels: 0 us -> 215 us
  blocking collectives: 63.4 us -> 0 us
  matrix products: 35.2 us -> 0 us
  between operations: 14.6 us -> 1.3 us
  other arithmetic: 11.8 us -> 0 us
  local copies, waits for them, and re-layouts: 6.59 us -> 1.67 us
  starting transfers between devices: 4.91 us -> 0 us
    all_gather x4 -> x0, waiting for transfers between devices: 281 us -> none  [the longest x3 241 us: side_by_side(): lax.all_gather(both, axis, axis=dim, tiled=True)]
    pallas_call x0 -> x1, Pallas kernels: none -> 215 us  [block(): pl.pallas_call(kernel, out_shape=jax.ShapeDtypeStruct(video.shape, video....]
    reduce_scatter x1 -> x0, waiting for transfers between devices: 64.8 us -> none  [local(): lax.psum_scatter(jnp.dot(attended, out_full, preferred_element_type=jnp.f...]
    all_to_all x3 -> x0, blocking collectives: 63.4 us -> none  [the longest x2 43.3 us: sent_to_all(): lax.all_to_all(jnp.broadcast_to(x[None], (devices, *x.shape)), axis, 0, 0...]
    dot_general x9 -> x0, matrix products: 33 us -> none  [the longest x3 12.7 us: video_path(): jnp.dot(whole_rows, blocks[index], preferred_element_type=jnp.float32)]
    concatenate x4 -> x0, other arithmetic: 4.99 us -> none  [the longest x3 4.24 us: side_by_side(): both = jnp.concatenate(arrays, axis=along)]
  transfers between devices with their start and end apart: 6 -> 0, of which waited for: 5 -> 0; matrix products, arithmetic and copies ran while one was open for 8% -> 0% of each run, Pallas kernels for 0% -> 0%
where the time goes in v1:
time: 219 us; the launch traced here: 218 us
  Pallas kernels  215 us (98%)
    pallas_call x1, Pallas kernels, block(): pl.pallas_call(kernel, out_shape=jax.ShapeDtypeStruct(video.shape, video....  215 us

profile of v1, /device:TPU:1, one launch (start us, length us, event | category | flops | bytes accessed | tf_op | source)
XLA Modules:
  0.0 217.7 jit_solution(4309723489665105265)
XLA Ops:
  1.3 214.7 %joint_attention.1 = bf16[1,32,4096]{2,1,0:T(8,128)(2,1)} custom-call(s32[1]{0:T(128)S(6)} %copy.19.length_ref, s32[16]{0:T(128)} %prompt_length_ref.1, s32[1]{0:T(128)S(6)} %copy.20.choice_ref, bf16[1,32,4096]{2,1,0:T(8,128)(2,1)} %video_ref.1, bf16[1,8,4096]{2,1,0:T(8,128)(2,1)} %prompt_ref.1, f32[1,4096]{1,0:T(1,128)} %bitcast.3, f32[1,4096]{1,0:T(1,128)} %bitcast.4, ...), custom_call_target="tpu_custom_call" | custom-call | tf_op jit(solution)/shard_map/joint_attention/pallas_call | solution.py:494
  216.0 1.7 copy.21

commit v2 on v1

--- a/solution.py
+++ b/solution.py
@@ -61,6 +61,10 @@
     keys,
     values,
     SB,
+    XR,
+    YR,
+    XS,
+    YS,
     RR,
     info_own,
     info,
@@ -73,6 +77,10 @@
     group_recv,
     group_send,
     group_send0,
+    video_recv,
+    video_send,
+    out_recv,
+    out_send,
 ):
     vid, seq = lax.axis_index("vid"), lax.axis_index("seq")
     yh, z = vid // 8, vid % 8
@@ -125,6 +133,10 @@
     row = lax.broadcasted_iota(jnp.int32, (8, 128), 0)
     text_live = prompt_length_ref[choice]
     info_own[...] = jnp.where(row == 0, choice, jnp.where(row == 1, length_ref[0], text_live))
+
+    normed = rms_norm(video_ref[0].astype(F32), video_gain_ref[...]).astype(BF)
+    NV[0] = normed[:, :2048]
+    NV[1] = normed[:, 2048:]
 
     pl.semaphore_wait(barrier, 33)
 
@@ -197,14 +209,92 @@
         ref = PB.at[pl.ds(0, 8)] if w == PROMPT else W.at[w, pl.ds(0, 8)]
         local(ref, ref, sib_recv.at[w]).wait()
 
+    not_diag = jnp.logical_not(diag)
+
+    def at_core(xk, yk, core):
+        return ((yk // 2) * 8 + z, xk * 4 + (yk % 2) * 2 + core)
+
+    def video_x(k):
+        return remote(
+            NV.at[0], XG.at[0, seq], video_send.at[0], video_recv.at[0], at_core((x + k) % 4, y, yh)
+        )
+
+    def video_y(k):
+        return remote(
+            NV.at[1], XG.at[1, seq], video_send.at[1], video_recv.at[1], at_core(x, (y + k) % 4, yh)
+        )
+
+    own_chip = [
+        remote(
+            NV.at[h], XG.at[h, seq], video_send.at[4], video_recv.at[h], sibling
+        )
+        for h in range(2)
+    ]
+
+    @pl.when(diag)
+    def _():
+        for h in range(2):
+            local(NV.at[h], XG.at[h, seq], video_recv.at[h]).start()
+
+    @pl.when(not_diag)
+    def _():
+        for h in range(2):
+            own_chip[h].start()
+
+    for k in (2, 1, 3):
+        video_x(k).start()
+        video_y(k).start()
+
+    def lower_piece(i):
+        return (i // 2) * 4 + yl * 2 + i % 2
+
+    def lower_on(i, k):
+        ref = XG.at[0, lower_piece(i)]
+        return remote(ref, ref, video_send.at[2], video_recv.at[2], at_core(x, (y + k) % 4, c))
+
+    def upper_on(k):
+        ref = XG.at[1, pl.ds(x * 4, 4)]
+        return remote(ref, ref, video_send.at[3], video_recv.at[3], at_core((x + k) % 4, y, c))
+
+    def pass_video_on():
+        ref = XG.at[1, pl.ds(0, 4)]
+        local(ref, ref, video_recv.at[1]).wait()
+        for k in (2, 1, 3):
+            upper_on(k).start()
+
+        @pl.when(diag)
+        def _():
+            ref = XG.at[0, pl.ds(0, 8)]
+            local(ref, ref, video_recv.at[0]).wait()
+
+            def step(i, carry):
+                for k in (2, 1, 3):
+                    lower_on(i, k).start()
+                return carry
+
+            lax.fori_loop(0, 8, step, 0)
+
+    def video_wait():
+        ref = XG.at[1, pl.ds(0, 12)]
+        local(ref, ref, video_recv.at[3]).wait()
+
+        @pl.when(diag)
+        def _():
+            ref = XG.at[0, pl.ds(0, 8)]
+            local(ref, ref, video_recv.at[2]).wait()
+
+        @pl.when(not_diag)
+        def _():
+            ref = XG.at[0]
+            local(ref, ref, video_recv.at[2]).wait()
+
     own(PROMPT)
     own(TK)
     own(TV)
 
-    NV[...] = rms_norm(video_ref[0].astype(F32), video_gain_ref[...]).astype(BF)
-
     for k in range(1, 5):
         hop(PROMPT, k)
+    pass_video_on()
     hop(TK, 1)
     hop(TV, 1)
 
@@ -217,7 +307,7 @@
 
     SEL[...] = lax.fori_loop(0, 16, pick, jnp.zeros(SEL.shape, F32)).astype(BF)
 
-    PROMPTS, SUMS, TEXT, VIDEO, OUT = range(5)
+    PROMPTS, SUMS, TEXT = range(3)
 
     def send_prompt(k):
         return remote(
@@ -245,13 +335,6 @@
     )
     first_send(prompt0, local(SEL, PG.at[head_block], group_recv.at[PROMPTS]), PROMPTS)
     spread(1, 16, send_prompt)
-
-    def send_video(k):
-        return remote(NV, XG.at[seq], group_send.at[VIDEO], group_recv.at[VIDEO], to_chip(k))
-
-    video0 = remote(NV, XG.at[seq], group_send0.at[VIDEO], group_recv.at[VIDEO], to_chip(0))
-    first_send(video0, local(NV, XG.at[seq], group_recv.at[VIDEO]), VIDEO)
-    spread(1, 16, send_video)
 
     hop(TK, 2)
     hop(TV, 2)
@@ -333,15 +416,15 @@
     hop(V, 2)
     hop(O, 2)
 
-    local(XG, XG, group_recv.at[VIDEO]).wait()
+    video_wait()
     sibling_wait(Q)
     sibling_wait(K)
     q_acc[...] = jnp.zeros_like(q_acc)
     k_acc[...] = jnp.zeros_like(k_acc)
 
     def video_rows(j):
-        at = pl.ds(pl.multiple_of(j * 256, 256), 256)
-        return XG[:, :, at].reshape(512, 256)
+        at = pl.ds(pl.multiple_of((j % 8) * 256, 256), 256)
+        return XG[j // 8, :, :, at].reshape(512, 256)
 
     def query_key(j, carry):
         rows = video_rows(j)
@@ -389,18 +472,36 @@
     position = lax.broadcasted_iota(jnp.int32, (1, 640), 1)
     live = position < jnp.where(position < 512, info[1:2, 0:1], info[2:3, 0:1] + 512)
 
-    def send_out(block):
-        return remote(
-            SB.at[block], RR.at[head_block], group_send.at[OUT], group_recv.at[OUT], (c * 8 + z, block)
-        )
-
-    out0_local = local(SB.at[seq], RR.at[head_block], group_recv.at[OUT])
-    out0 = remote(
-        SB.at[seq], RR.at[head_block], group_send0.at[OUT], group_recv.at[OUT], (c * 8 + z, seq)
-    )
+    def out_x(part):
+        return remote(
+            SB.at[0, pl.ds(part * 4, 4)],
+            XR.at[(x + 3 - part) % 4],
+            out_send.at[0],
+            out_recv.at[0],
+            at_core(part, y, c),
+        )
+
+    def out_y(part, k):
+        return remote(
+            SB.at[1, pl.ds(part * 4 + k * 2, 2)],
+            YR.at[(y + 3 - (c * 2 + k)) % 4, pl.ds(part * 2, 2)],
+            out_send.at[1 + k],
+            out_recv.at[1],
+            at_core(x, c * 2 + k, c),
+        )
+
+    def sum_x(k):
+        return remote(
+            XS.at[k], RR.at[0, y], out_send.at[3 + k], out_recv.at[2], at_core(x, c * 2 + k // 2, k % 2)
+        )
+
+    def sum_y(xk, core, send):
+        return remote(
+            YS.at[xk * 2 + core], RR.at[1, x], send, out_recv.at[3], at_core(xk, y, core)
+        )
 
     def attend(i, carry):
-        part = (x + i) % 4
+        part = (x + 1 + i) % 4
         rows = pl.ds(pl.multiple_of(part * 128, 128), 128)
         heads = []
         for h in range(2):
@@ -416,55 +517,117 @@
 
         for j in range(16):
             projected = jnp.dot(attended, W[O, j], preferred_element_type=F32)
-            SB[pl.ds(part * 4, 4), :, pl.ds(j * 256, 256)] = projected.reshape(4, 32, 256).astype(BF)
-
-        def send(k, carry):
-            block = part * 4 + (seq + k) % 4
-
-            @pl.when(block != seq)
+            SB[j // 8, pl.ds(part * 4, 4), :, pl.ds((j % 8) * 256, 256)] = projected.reshape(4, 32, 256).astype(BF)
+
+        @pl.when(part != x)
+        def _():
+            out_x(part).start()
+
+        for k in range(2):
+
+            @pl.when(y != c * 2 + k)
             def _():
-                send_out(block).start()
-
-            @pl.when(block == seq)
+                out_y(part, k).start()
+
+        return carry
+
+    lax.fori_loop(0, 4, attend, 0)
+
+    local(XR, XR, out_recv.at[0]).wait()
+    for k in range(4):
+        for lanes in (pl.ds(0, 1024), pl.ds(1024, 1024)):
+            total = SB[0, x * 4 + k, :, lanes].astype(F32)
+            for i in range(3):
+                total = total + XR[i, k, :, lanes].astype(F32)
+            XS[k, :, lanes] = total.astype(BF)
+        to_here = jnp.logical_and(diag, jnp.logical_and(yl == k // 2, c == k % 2))
+
+        @pl.when(to_here)
+        def _():
+            local(XS.at[k], RR.at[0, y], out_recv.at[2]).start()
+
+        @pl.when(jnp.logical_not(to_here))
+        def _():
+            sum_x(k).start()
+
+    @pl.when(diag)
+    def _():
+        local(YR, YR, out_recv.at[1]).wait()
+
+        def step(i, carry):
+            xk, core = (x + 1 + i // 2) % 4, (c + 1 + i) % 2
+            for lanes in (pl.ds(0, 1024), pl.ds(1024, 1024)):
+                total = SB[1, xk * 4 + yl * 2 + core, :, lanes].astype(F32)
+                for j in range(3):
+                    total = total + YR[j, xk * 2 + core, :, lanes].astype(F32)
+                YS[xk * 2 + core, :, lanes] = total.astype(BF)
+
+            @pl.when(i < 7)
             def _():
-                first_send(out0, out0_local, OUT)
+                sum_y(xk, core, out_send.at[7]).start()
+
+            @pl.when(i == 7)
+            def _():
+                local(YS.at[xk * 2 + core], RR.at[1, x], out_recv.at[3]).start()
 
             return carry
 
-        lax.fori_loop(0, 4, send, 0)
-        return carry
-
-    lax.fori_loop(0, 4, attend, 0)
-
-    local(RR, RR, group_recv.at[OUT]).wait()
+        lax.fori_loop(0, 8, step, 0)
+
+    local(RR.at[0], RR.at[0], out_recv.at[2]).wait()
+    local(RR.at[1], RR.at[1], out_recv.at[3]).wait()
     row_position = seq * 32 + lax.broadcasted_iota(jnp.int32, (32, 1), 0)
     row_live = row_position < length_ref[0]
 
-    def add_up(j, carry):
-        at = pl.ds(pl.multiple_of(j * 512, 512), 512)
-        total = RR[0, :, at].astype(F32)
-        for i in range(1, 16):
-            total = total + RR[i, :, at].astype(F32)
-        updated = video_ref[0, :, at].astype(F32) + jnp.where(row_live, total, 0.0)
-        out_ref[0, :, at] = updated.astype(BF)
-        return carry
-
-    lax.fori_loop(0, 8, add_up, 0)
+    for half in range(2):
+        for j in range(4):
+            at = pl.ds(j * 512, 512)
+            total = RR[half, 0, :, at].astype(F32)
+            for i in range(1, 4):
+                total = total + RR[half, i, :, at].astype(F32)
+            at = pl.ds(half * 2048 + j * 512, 512)
+            updated = video_ref[0, :, at].astype(F32) + jnp.where(row_live, total, 0.0)
+            out_ref[0, :, at] = updated.astype(BF)
 
     @pl.when(jnp.logical_not(diag))
     def _():
         for w in range(7):
             swap_copy(w).wait_send()
         info_copy.wait_send()
-        for group, copy in ((PROMPTS, prompt0), (TEXT, text0), (VIDEO, video0), (OUT, out0)):
-            copy.wait_send()
+        prompt0.wait_send()
+        text0.wait_send()
+        both = XG.at[0, pl.ds(0, 2)]
+        local(both, both, video_send.at[4]).wait()
 
     for w in range(7):
         ref = PB.at[pl.ds(0, 15)] if w == PROMPT else W.at[w, pl.ds(0, 15)]
         local(ref, ref, ring_send.at[w]).wait()
-    for group, buffer in ((PROMPTS, PG), (SUMS, FR), (TEXT, TG), (VIDEO, XG), (OUT, RR)):
+    for group, buffer in ((PROMPTS, PG), (SUMS, FR), (TEXT, TG)):
         ref = buffer.at[pl.ds(0, 15)]
         local(ref, ref, group_send.at[group]).wait()
+    for sem, pieces in ((video_send.at[0], 3), (video_send.at[1], 3), (video_send.at[3], 12), (out_send.at[0], 12)):
+        ref = XG.at[0, pl.ds(0, pieces)]
+        local(ref, ref, sem).wait()
+    for k in range(2):
+
+        @pl.when(y != c * 2 + k)
+        def _():
+            ref = XG.at[0, pl.ds(0, 8)]
+            local(ref, ref, out_send.at[1 + k]).wait()
+
+    for k in range(4):
+        to_here = jnp.logical_and(diag, jnp.logical_and(yl == k // 2, c == k % 2))
+
+        @pl.when(jnp.logical_not(to_here))
+        def _():
+            sum_x(k).wait_send()
+
+    @pl.when(diag)
+    def _():
+        ref = XG.reshape(32, 32, 2048).at[pl.ds(0, 24)]
+        local(ref, ref, video_send.at[2]).wait()
+        ref = YS.at[pl.ds(0, 7)]
+        local(ref, ref, out_send.at[7]).wait()
 
 
 def block(
@@ -490,7 +653,7 @@
     vmem = pl.BlockSpec(memory_space=pltpu.VMEM)
     hbm = pl.BlockSpec(memory_space=pl.ANY)
     dma = pltpu.SemaphoreType.DMA
-    width = 4096
+    width, half = 4096, 2048
     return pl.pallas_call(
         kernel,
         out_shape=jax.ShapeDtypeStruct(video.shape, video.dtype),
@@ -512,16 +675,20 @@
             pltpu.VMEM((16, 8, width), BF),
             pltpu.VMEM((8, width), BF),
             pltpu.VMEM((16, 8, width), BF),
-            pltpu.VMEM((32, width), BF),
-            pltpu.VMEM((16, 32, width), BF),
+            pltpu.VMEM((2, 32, half), BF),
+            pltpu.VMEM((2, 16, 32, half), BF),
             pltpu.VMEM((512, 256), F32),
             pltpu.VMEM((512, 256), F32),
             pltpu.VMEM((512, 256), F32),
             pltpu.VMEM((512, 256), BF),
             pltpu.VMEM((640, 256), BF),
             pltpu.VMEM((640, 256), BF),
-            pltpu.VMEM((16, 32, width), BF),
-            pltpu.VMEM((16, 32, width), BF),
+            pltpu.VMEM((2, 16, 32, half), BF),
+            pltpu.VMEM((3, 4, 32, half), BF),
+            pltpu.VMEM((3, 8, 32, half), BF),
+            pltpu.VMEM((4, 32, half), BF),
+            pltpu.VMEM((8, 32, half), BF),
+            pltpu.VMEM((2, 4, 32, half), BF),
             pltpu.VMEM((8, 128), jnp.int32),
             pltpu.VMEM((8, 128), jnp.int32),
             dma((3,)),
@@ -530,9 +697,13 @@
             dma((8,)),
             dma((7,)),
             dma,
+            dma((3,)),
+            dma((3,)),
+            dma((3,)),
+            dma((4,)),
             dma((5,)),
-            dma((5,)),
-            dma((5,)),
+            dma((4,)),
+            dma((8,)),
         ],
         compiler_params=pltpu.CompilerParams(
             collective_id=0, has_side_effects=True, vmem_limit_bytes=58 * 1024 * 1024

time: 219 us -> 159 us (0.73)
  Pallas kernels: 215 us -> 156 us
    pallas_call x1, Pallas kernels: 215 us -> 156 us  [block(): pl.pallas_call(kernel, out_shape=jax.ShapeDtypeStruct(video.shape, video....]
where the time goes in v2:
time: 159 us
  Pallas kernels  156 us (98%)
  local copies, waits for them, and re-layouts  1.67 us (1%)
    pallas_call x1, Pallas kernels, block(): pl.pallas_call(kernel, out_shape=jax.ShapeDtypeStruct(video.shape, video....  156 us

profile of v2, /device:TPU:1, one launch (start us, length us, event | category | flops | bytes accessed | tf_op | source)
XLA Modules:
  0.0 158.7 jit_solution(1203180292903282827)
XLA Ops:
  1.3 155.8 %joint_attention.1 = bf16[1,32,4096]{2,1,0:T(8,128)(2,1)} custom-call(s32[1]{0:T(128)S(6)} %copy.19.length_ref, s32[16]{0:T(128)} %prompt_length_ref.1, s32[1]{0:T(128)S(6)} %copy.20.choice_ref, bf16[1,32,4096]{2,1,0:T(8,128)(2,1)} %video_ref.1, bf16[1,8,4096]{2,1,0:T(8,128)(2,1)} %prompt_ref.1, f32[1,4096]{1,0:T(1,128)} %bitcast.3, f32[1,4096]{1,0:T(1,128)} %bitcast.4, ...), custom_call_target="tpu_custom_call" | custom-call | tf_op jit(solution)/shard_map/joint_attention/pallas_call | solution.py:657
  157.1 1.7 %copy.21 = bf16[1,32,4096]{2,1,0:T(8,128)(2,1)} copy(bf16[1,32,4096]{2,1,0:T(8,128)(2,1)} %joint_attention.1) | data formatting | bytes 524288

commit v3 on v2

v3 whole, which is shorter than its diff:
```python
import jax
import jax.numpy as jnp
from jax import lax
from jax.experimental import pallas as pl
from jax.experimental.pallas import tpu as pltpu
from jax.sharding import PartitionSpec as P

HD = 128
EPSILON = 1e-06
MESH = pl.DeviceIdType.MESH
BF = jnp.bfloat16
F32 = jnp.float32

TK, TV, Q, K, V, O, PROMPT = range(7)


def rms_norm(values, gain):
    return values * lax.rsqrt(jnp.mean(values * values, axis=-1, keepdims=True) + EPSILON) * gain


def kernel(
    length_ref,
    prompt_length_ref,
    choice_ref,
    video_ref,
    prompt_ref,
    ffn_gain_ref,
    final_gain_ref,
    video_gain_ref,
    gate_hbm,
    up_hbm,
    down_hbm,
    w_text_key,
    w_text_value,
    w_query,
    w_key,
    w_value,
    w_out,
    out_ref,
    W,
    PB,
    SEL,
    PG,
    FN,
    gate_ref,
    up_ref,
    down_ref,
    gate_acc,
    up_acc,
    hidden,
    FP,
    FS,
    FQ,
    FR,
    TX,
    TG,
    NV,
    XG,
    q_acc,
    k_acc,
    v_acc,
    queries,
    probs,
    keys,
    values,
    AX,
    OX,
    SB,
    YR,
    YS,
    RR,
    info_own,
    info,
    ffn_sem,
    ring_recv,
    ring_send,
    swap_send,
    sib_recv,
    info_sem,
    group_recv,
    group_send,
    group_send0,
    prompt_sem,
    video_recv,
    video_send,
    out_recv,
    out_send,
    weight_sem,
    weight_recv,
):
    vid, seq = lax.axis_index("vid"), lax.axis_index("seq")
    yh, z = vid // 8, vid % 8
    x, yl, c = seq // 4, (seq // 2) % 2, seq % 2
    y = yh * 2 + yl
    diag = c == yh
    taken = (y + 3) % 4
    head_block = x * 4 + (taken % 2) * 2 + taken // 2
    taker = (yl + 1 + 2 * c) % 4
    taker = ((taker // 2) * 8 + z, x * 4 + (taker % 2) * 2 + yh)
    sibling = (vid, seq + 1 - 2 * c)
    z_right = (yh * 8 + (z + 1) % 8, seq)
    z_left = (yh * 8 + (z + 7) % 8, seq)

    def to_chip(k):
        xk, yk = (x + k // 4) % 4, (y + k % 4) % 4
        return ((yk // 2) * 8 + z, xk * 4 + (yk % 2) * 2 + yh)

    def place(k):
        return ((x + k // 4) % 4) * 4 + ((yl + (k // 2) % 2) % 2) * 2 + (c + k % 2) % 2

    def local(src, dst, sem):
        return pltpu.make_async_copy(src, dst, sem)

    def remote(src, dst, send, recv, device):
        return pltpu.make_async_remote_copy(
            src_ref=src, dst_ref=dst, send_sem=send, recv_sem=recv, device_id=device, device_id_type=MESH
        )

    ffn_copies = [
        local(gate_hbm, gate_ref, ffn_sem.at[0]),
        local(up_hbm, up_ref, ffn_sem.at[1]),
        local(down_hbm, down_ref, ffn_sem.at[2]),
    ]
    for copy in ffn_copies:
        copy.start()

    barrier = pltpu.get_barrier_semaphore()

    def greet(k, carry):
        seq_k = (seq + k) % 16
        vid_k = ((yh + k // 16) % 2) * 8 + z
        pl.semaphore_signal(barrier, inc=1, device_id=(vid_k, seq_k), device_id_type=MESH)
        return carry

    lax.fori_loop(1, 32, greet, 0)
    for neighbour in (z_left, z_right):
        pl.semaphore_signal(barrier, inc=1, device_id=neighbour, device_id_type=MESH)

    choice = choice_ref[0]
    row = lax.broadcasted_iota(jnp.int32, (8, 128), 0)
    text_live = prompt_length_ref[choice]
    info_own[...] = jnp.where(row == 0, choice, jnp.where(row == 1, length_ref[0], text_live))

    normed = rms_norm(video_ref[0].astype(F32), video_gain_ref[...]).astype(BF)
    NV[0] = normed[:, :2048]
    NV[1] = normed[:, 2048:]

    pl.semaphore_wait(barrier, 33)

    sources = [w_text_key, w_text_value, w_query, w_key, w_value, w_out, prompt_ref.at[0]]

    def slot(w, block):
        return PB.at[block] if w == PROMPT else W.at[w, block]

    def swap_copy(w):
        return remote(sources[w], slot(w, yh * 8 + z), swap_send.at[w], ring_recv.at[w, z], taker)

    info_copy = remote(info_own, info, swap_send.at[7], info_sem, taker)
    swap_copy(PROMPT).start()
    info_copy.start()

    def swap(w):
        swap_copy(w).start()

    def ring_wait(w, zz):
        ref = slot(w, c * 8 + zz)
        local(ref, ref, ring_recv.at[w, zz]).wait()

    def ring_to(w, zz, device):
        ref = slot(w, c * 8 + zz)
        remote(ref, ref, ring_send.at[w], ring_recv.at[w, zz], device).start()

    def to_sibling(w, zz):
        if w in (O, PROMPT):
            return
        ref = slot(w, c * 8 + zz)
        remote(ref, ref, ring_send.at[w], sib_recv.at[w], sibling).start()

    def own(w):
        ring_wait(w, z)
        ring_to(w, z, z_right)
        ring_to(w, z, z_left)
        to_sibling(w, z)

    def hop(w, k):
        right_hops = 4 if w % 2 == 0 else 3
        left_hops = 7 - right_hops
        from_left, from_right = (z + 8 - k) % 8, (z + k) % 8
        if k <= right_hops:
            ring_wait(w, from_left)
            if k < right_hops:
                ring_to(w, from_left, z_right)
        if k <= left_hops:
            ring_wait(w, from_right)
            if k < left_hops:
                ring_to(w, from_right, z_left)
        if k <= right_hops:
            to_sibling(w, from_left)
        if k <= left_hops:
            to_sibling(w, from_right)

    def sibling_wait(w):
        ref = W.at[w, pl.ds(0, 8)]
        local(ref, ref, sib_recv.at[w]).wait()

    not_diag = jnp.logical_not(diag)

    def at_core(xk, yk, core):
        return ((yk // 2) * 8 + z, xk * 4 + (yk % 2) * 2 + core)

    def video_slot(h):
        return XG.at[h, x, yl, c]

    def video_x(k):
        return remote(
            NV.at[0], video_slot(0), video_send.at[0], video_recv.at[0], at_core((x + k) % 4, y, yh)
        )

    def video_y(k):
        return remote(
            NV.at[1], video_slot(1), video_send.at[1], video_recv.at[1], at_core(x, (y + k) % 4, yh)
        )

    own_chip = [
        remote(
            NV.at[h], video_slot(h), video_send.at[4], video_recv.at[h], sibling
        )
        for h in range(2)
    ]

    @pl.when(diag)
    def _():
        for h in range(2):
            local(NV.at[h], video_slot(h), video_recv.at[h]).start()

    @pl.when(not_diag)
    def _():
        for h in range(2):
            own_chip[h].start()

    def send_lower():
        for k in (2, 1, 3):
            video_x(k).start()

    def send_upper():
        for k in (2, 1, 3):
            video_y(k).start()

    def lower_on(k):
        ref = XG.at[0, :, yl]
        return remote(ref, ref, video_send.at[2], video_recv.at[2], at_core(x, (y + k) % 4, c))

    def upper_on(k):
        ref = XG.at[1, x]
        return remote(ref, ref, video_send.at[3], video_recv.at[3], at_core((x + k) % 4, y, c))

    def pass_upper_on():
        ref = XG.at[1, 0]
        local(ref, ref, video_recv.at[1]).wait()
        for k in (2, 1, 3):
            upper_on(k).start()

    def pass_lower_on():
        @pl.when(diag)
        def _():
            ref = XG.at[0, pl.ds(0, 2)]
            local(ref, ref, video_recv.at[0]).wait()
            for k in (2, 1, 3):
                lower_on(k).start()

    def video_wait():
        ref = XG.at[1, pl.ds(0, 3)]
        local(ref, ref, video_recv.at[3]).wait()

        @pl.when(diag)
        def _():
            ref = XG.at[0, pl.ds(0, 2)]
            local(ref, ref, video_recv.at[2]).wait()

        @pl.when(not_diag)
        def _():
            ref = XG.at[0]
            local(ref, ref, video_recv.at[2]).wait()

    PROMPTS, SUMS, TEXT = range(3)

    def send_prompt(k):
        device = (c * 8 + z, ((x + k // 2) % 4) * 4 + ((yl + k % 2) % 2) * 2 + x // 2)
        return remote(SEL, PG.at[head_block], group_send.at[PROMPTS], group_recv.at[PROMPTS], device)

    half_chosen = PG.at[pl.ds(pl.multiple_of(c * 8, 8), 8)]
    pass_chosen = remote(half_chosen, half_chosen, prompt_sem.at[2], prompt_sem.at[3], sibling)

    def pass_chosen_on():
        local(half_chosen, half_chosen, group_recv.at[PROMPTS]).wait()
        pass_chosen.start()

    def spread(first, last, make):
        def step(k, carry):
            make(k).start()
            return carry

        lax.fori_loop(first, last, step, 0)

    def first_send(copy, copy_local, group):
        @pl.when(diag)
        def _():
            copy_local.start()

        @pl.when(jnp.logical_not(diag))
        def _():
            copy.start()

    prompt0 = remote(
        SEL,
        PG.at[head_block],
        group_send0.at[PROMPTS],
        group_recv.at[PROMPTS],
        (c * 8 + z, x * 4 + yl * 2 + x // 2),
    )
    chosen_here = jnp.logical_and(diag, c == x // 2)

    def send_prompts():
        ring_wait(PROMPT, z)
        ref = PB.at[c * 8 + z]

        def step(k, carry):
            remote(
                ref, ref, ring_send.at[PROMPT], sib_recv.at[PROMPT], (yh * 8 + (z + k) % 8, seq)
            ).start()
            return carry

        lax.fori_loop(1, 8, step, 0)

    half_prompts = PB.at[pl.ds(pl.multiple_of(c * 8, 8), 8)]
    pass_prompts = remote(half_prompts, half_prompts, prompt_sem.at[0], prompt_sem.at[1], sibling)

    def pass_prompts_on():
        ref = PB.at[pl.ds(0, 7)]
        local(ref, ref, sib_recv.at[PROMPT]).wait()
        pass_prompts.start()

    def choose_prompt():
        pass_prompts.wait_recv()
        local(info, info, info_sem).wait()
        wanted = info[0:1, 0:1]

        def pick(i, total):
            return total + jnp.where(wanted == i, PB[i].astype(F32), 0.0)

        SEL[...] = lax.fori_loop(0, 16, pick, jnp.zeros(SEL.shape, F32)).astype(BF)

        @pl.when(chosen_here)
        def _():
            local(SEL, PG.at[head_block], group_recv.at[PROMPTS]).start()

        @pl.when(jnp.logical_not(chosen_here))
        def _():
            prompt0.start()

        spread(1, 8, send_prompt)

    def norm_rows(i, carry):
        rows = PG[pl.ds(2 * i, 2)].astype(F32).reshape(16, PG.shape[2])
        FN[pl.ds(pl.multiple_of(i * 16, 16), 16), :] = rms_norm(rows, ffn_gain_ref[...]).astype(BF)
        return carry

    def gate_up(i, carry):
        at = pl.ds(pl.multiple_of(i * 512, 512), 512)
        rows = FN[:, at]
        gate_acc[...] += jnp.dot(rows, gate_ref[at, :], preferred_element_type=F32)
        up_acc[...] += jnp.dot(rows, up_ref[at, :], preferred_element_type=F32)
        return carry

    def ffn_up():
        pass_chosen.wait_recv()
        lax.fori_loop(0, 8, norm_rows, 0)
        ffn_copies[0].wait()
        ffn_copies[1].wait()
        gate_acc[...] = jnp.zeros_like(gate_acc)
        up_acc[...] = jnp.zeros_like(up_acc)
        lax.fori_loop(0, 8, gate_up, 0)
        hidden[...] = (jax.nn.gelu(gate_acc[...], approximate=True) * up_acc[...]).astype(BF)

    def down_proj(i, carry):
        at = pl.ds(pl.multiple_of(i * 256, 256), 256)
        part = jnp.dot(hidden[...], down_ref[:, at], preferred_element_type=F32)
        FP[:, :, :, at] = part.reshape(8, 2, 8, 256).astype(BF)
        return carry

    pass_sums = remote(FP.at[:, 1 - c], FS, prompt_sem.at[4], prompt_sem.at[5], sibling)
    own_chip_index = seq // 2

    def send_sums(k):
        to = ((x + k // 2) % 4) * 2 + (yl + k % 2) % 2
        return remote(
            FQ.at[to], FR.at[own_chip_index], group_send.at[SUMS], group_recv.at[SUMS], (vid, to * 2 + c)
        )

    def ffn_down():
        ffn_copies[2].wait()
        lax.fori_loop(0, 16, down_proj, 0)
        pass_sums.start()

    def ffn_sums():
        pass_sums.wait_recv()

        def step(i, carry):
            FQ[i] = (FP[i, c].astype(F32) + FS[i].astype(F32)).astype(BF)
            return carry

        lax.fori_loop(0, 8, step, 0)
        local(FQ.at[own_chip_index], FR.at[own_chip_index], group_recv.at[SUMS]).start()
        spread(1, 8, send_sums)

    def send_text(k):
        return remote(TX, TG.at[seq], group_send.at[TEXT], group_recv.at[TEXT], to_chip(k))

    text0 = remote(TX, TG.at[seq], group_send0.at[TEXT], group_recv.at[TEXT], to_chip(0))

    def text_rows():
        local(FR, FR, group_recv.at[SUMS]).wait()
        encoded = lax.fori_loop(
            0, 8, lambda i, total: total + FR[i].astype(F32), jnp.zeros(TX.shape, F32)
        )
        encoded = PG[seq].astype(F32) + encoded
        TX[...] = rms_norm(encoded, final_gain_ref[...]).astype(BF)
        first_send(text0, local(TX, TG.at[seq], group_recv.at[TEXT]), TEXT)
        spread(1, 16, send_text)

    def video_rows(j):
        at = pl.ds(pl.multiple_of((j % 8) * 256, 256), 256)
        return XG[j // 8, :, :, :, :, at].reshape(512, 256)

    def project(w, acc, result):
        sibling_wait(w)
        acc[...] = jnp.zeros_like(acc)

        def step(j, carry):
            acc[...] += jnp.dot(video_rows(j), W[w, j], preferred_element_type=F32)
            return carry

        lax.fori_loop(0, 16, step, 0)
        result[pl.ds(0, 512), :] = acc[...].astype(BF)

    def text_key_value(j, carry):
        at = pl.ds(pl.multiple_of(j * 256, 256), 256)
        rows = TG[:, :, at].astype(F32).reshape(128, 256).astype(BF)
        key_sum, value_sum = carry
        key_sum = key_sum + jnp.dot(rows, W[TK, j], preferred_element_type=F32)
        value_sum = value_sum + jnp.dot(rows, W[TV, j], preferred_element_type=F32)
        return key_sum, value_sum

    def text_projections():
        local(TG, TG, group_recv.at[TEXT]).wait()
        sibling_wait(TK)
        sibling_wait(TV)
        zero = jnp.zeros((128, 256), F32)
        text_key, text_value = lax.fori_loop(0, 16, text_key_value, (zero, zero))
        keys[pl.ds(512, 128), :] = text_key.astype(BF)
        values[pl.ds(512, 128), :] = text_value.astype(BF)

    mine = x // 2 == c

    def weight_copy(i):
        xk = 2 * c + i
        return remote(
            W.at[O, pl.ds(pl.multiple_of(xk * 4, 4), 4)], OX.at[x], weight_sem.at[i], weight_recv, at_core(xk, y, c)
        )

    def send_weights():
        for i in range(2):

            @pl.when(x != 2 * c + i)
            def _():
                weight_copy(i).start()

            @pl.when(x == 2 * c + i)
            def _():
                local(W.at[O, pl.ds(pl.multiple_of(x * 4, 4), 4)], OX.at[x], weight_recv).start()

    pass_weights = remote(OX, OX, weight_sem.at[2], weight_sem.at[3], sibling)

    def pass_weights_on():
        @pl.when(mine)
        def _():
            local(OX, OX, weight_recv).wait()
            pass_weights.start()

    def weights_wait():
        @pl.when(jnp.logical_not(mine))
        def _():
            pass_weights.wait_recv()

    def attended_x(part, xk):
        ref = AX.at[x, part]
        return remote(ref, ref, out_send.at[0], out_recv.at[part], at_core(xk, y, c))

    def out_y(part, k):
        return remote(
            SB.at[pl.ds(part * 4 + k * 2, 2)],
            YR.at[(y + 3 - (c * 2 + k)) % 4, pl.ds(part * 2, 2)],
            out_send.at[1 + k],
            out_recv.at[4 + part],
            at_core(x, c * 2 + k, c),
        )

    def sum_y(xk, core):
        return remote(
            YS.at[xk * 2 + core], RR.at[x], out_send.at[3], out_recv.at[8], at_core(xk, y, core)
        )

    def attention_probs(first, last):
        position = lax.broadcasted_iota(jnp.int32, (1, 640), 1)
        live = position < jnp.where(position < 512, info[1:2, 0:1], info[2:3, 0:1] + 512)

        def step(i, carry):
            part = (x + 1 + i) % 4
            rows = pl.ds(pl.multiple_of(part * 128, 128), 128)
            for h in range(2):
                lanes = pl.ds(h * HD, HD)
                scores = lax.dot_general(
                    queries[rows, lanes], keys[:, lanes], (((1,), (1,)), ((), ())), preferred_element_type=F32
                )
                scores = jnp.where(live, scores * HD ** (-0.5), -1e30)
                e = jnp.exp(scores - jnp.max(scores, axis=-1, keepdims=True))
                probs[part, h] = (e / jnp.sum(e, axis=-1, keepdims=True)).astype(BF)
            return carry

        lax.fori_loop(first, last, step, 0)

    def attend(part, carry):
        for h in range(2):
            lanes = pl.ds(h * HD, HD)
            AX[x, part, :, lanes] = jnp.dot(
                probs[part, h], values[:, lanes], preferred_element_type=F32
            ).astype(BF)
        return carry

    def attend_all():
        lax.fori_loop(0, 4, attend, 0)

        def step(i, carry):
            for k in (2, 1, 3):
                xk = (x + k) % 4
                attended_x((xk + 1 + i) % 4, xk).start()
            return carry

        lax.fori_loop(0, 4, step, 0)

    def project_part(i, carry):
        part = (x + 1 + i) % 4
        ref = AX.at[pl.ds(0, 3), 0]
        local(ref, ref, out_recv.at[part]).wait()
        for m in range(4):
            total = jnp.dot(AX[0, part], OX[0, m], preferred_element_type=F32)
            for j in range(1, 4):
                total = total + jnp.dot(AX[j, part], OX[j, m], preferred_element_type=F32)
            SB[pl.ds(part * 4, 4), :, pl.ds(m * 256, 256)] = total.reshape(4, 32, 256).astype(BF)
        for k in range(2):

            @pl.when(y != c * 2 + k)
            def _():
                out_y(part, k).start()

        return carry

    def sum_part(i, carry):
        part = (x + 1 + i) % 4
        ref = YR.at[pl.ds(0, 3), pl.ds(0, 2)]
        local(ref, ref, out_recv.at[4 + part]).wait()
        for step in range(2):
            core = (c + 1 + step) % 2
            total = SB[part * 4 + yl * 2 + core].astype(F32)
            for j in range(3):
                total = total + YR[j, part * 2 + core].astype(F32)
            YS[part * 2 + core] = total.astype(BF)
            to_here = jnp.logical_and(part == x, core == c)

            @pl.when(jnp.logical_not(to_here))
            def _():
                sum_y(part, core).start()

            @pl.when(to_here)
            def _():
                local(YS.at[part * 2 + core], RR.at[x], out_recv.at[8]).start()

        return carry

    send_lower()
    swap(TK)
    send_upper()
    own(PROMPT)
    swap(TV)
    own(TK)
    hop(PROMPT, 1)
    swap(O)
    own(TV)
    hop(PROMPT, 2)
    swap(Q)
    hop(PROMPT, 3)
    own(O)
    swap(K)
    hop(PROMPT, 4)
    pass_prompts.start()
    own(Q)
    hop(TK, 1)
    choose_prompt()
    swap(V)
    hop(TV, 1)
    hop(O, 1)
    hop(Q, 1)
    own(K)
    own(V)
    pass_chosen_on()
    pass_upper_on()
    pass_lower_on()
    ffn_up()
    hop(TK, 2)
    hop(TV, 2)
    hop(O, 2)
    hop(Q, 2)
    hop(K, 1)
    ffn_down()
    hop(V, 1)
    hop(TK, 3)
    ffn_sums()
    hop(TV, 3)
    hop(O, 3)
    hop(Q, 3)
    hop(K, 2)
    hop(V, 2)
    text_rows()
    hop(TK, 4)
    hop(TV, 4)
    hop(O, 4)
    hop(Q, 4)
    hop(K, 3)
    hop(V, 3)
    send_weights()
    video_wait()
    project(Q, q_acc, queries)
    hop(K, 4)
    project(K, k_acc, keys)
    text_projections()
    attention_probs(0, 4)
    pass_weights_on()
    hop(V, 4)
    project(V, v_acc, values)
    attend_all()
    weights_wait()
    lax.fori_loop(0, 4, project_part, 0)

    @pl.when(diag)
    def _():
        lax.fori_loop(0, 4, sum_part, 0)

    local(RR, RR, out_recv.at[8]).wait()
    row_position = seq * 32 + lax.broadcasted_iota(jnp.int32, (32, 1), 0)
    row_live = row_position < length_ref[0]

    for j in range(4):
        at = pl.ds(j * 1024, 1024)
        updated = video_ref[0, :, at].astype(F32) + jnp.where(row_live, RR[j].astype(F32), 0.0)
        out_ref[0, :, at] = updated.astype(BF)

    for w in range(7):
        swap_copy(w).wait_send()
    info_copy.wait_send()

    @pl.when(jnp.logical_not(diag))
    def _():
        text0.wait_send()
        both = XG.at[0, 0, 0]
        local(both, both, video_send.at[4]).wait()

    pass_prompts.wait_send()
    for w in range(7):
        ref = PB.at[pl.ds(0, 7)] if w == PROMPT else W.at[w, pl.ds(0, 7 if w == O else 15)]
        local(ref, ref, ring_send.at[w]).wait()
    @pl.when(jnp.logical_not(chosen_here))
    def _():
        prompt0.wait_send()

    pass_chosen.wait_send()
    pass_sums.wait_send()
    for group, buffer in ((PROMPTS, PG), (SUMS, FR), (TEXT, TG)):
        ref = buffer.at[pl.ds(0, 15 if group == TEXT else 7)]
        local(ref, ref, group_send.at[group]).wait()
    for sem in (video_send.at[0], video_send.at[1]):
        ref = XG.at[0, pl.ds(0, 3), 0, 0]
        local(ref, ref, sem).wait()
    ref = XG.at[0, pl.ds(0, 3)]
    local(ref, ref, video_send.at[3]).wait()
    ref = AX.at[pl.ds(0, 3)]
    local(ref, ref, out_send.at[0]).wait()
    for k in range(2):

        @pl.when(x != 2 * c + k)
        def _():
            weight_copy(k).wait_send()

        @pl.when(y != c * 2 + k)
        def _():
            ref = SB.at[pl.ds(0, 8)]
            local(ref, ref, out_send.at[1 + k]).wait()

    @pl.when(mine)
    def _():
        pass_weights.wait_send()

    @pl.when(diag)
    def _():
        ref = XG.at[:, pl.ds(0, 3)]
        local(ref, ref, video_send.at[2]).wait()
        ref = YS.at[pl.ds(0, 7)]
        local(ref, ref, out_send.at[3]).wait()


def block(
    video,
    video_length,
    prompt,
    prompt_length,
    prompt_choice,
    ffn_gain,
    ffn_gate,
    ffn_up,
    ffn_down,
    final_gain,
    video_gain,
    w_query,
    w_key,
    w_value,
    w_text_key,
    w_text_value,
    w_out,
):
    smem = pl.BlockSpec(memory_space=pltpu.SMEM)
    vmem = pl.BlockSpec(memory_space=pltpu.VMEM)
    hbm = pl.BlockSpec(memory_space=pl.ANY)
    dma = pltpu.SemaphoreType.DMA
    width, half, quarter = 4096, 2048, 1024
    return pl.pallas_call(
        kernel,
        out_shape=jax.ShapeDtypeStruct(video.shape, video.dtype),
        in_specs=[smem] * 3 + [vmem] * 5 + [hbm] * 9,
        out_specs=vmem,
        scratch_shapes=[
            pltpu.VMEM((6, 16, 256, 256), BF),
            pltpu.VMEM((16, 8, width), BF),
            pltpu.VMEM((8, width), BF),
            pltpu.VMEM((16, 8, width), BF),
            pltpu.VMEM((128, width), BF),
            pltpu.VMEM(ffn_gate.shape, BF),
            pltpu.VMEM(ffn_up.shape, BF),
            pltpu.VMEM(ffn_down.shape, BF),
            pltpu.VMEM((128, 384), F32),
            pltpu.VMEM((128, 384), F32),
            pltpu.VMEM((128, 384), BF),
            pltpu.VMEM((8, 2, 8, width), BF),
            pltpu.VMEM((8, 8, width), BF),
            pltpu.VMEM((8, 8, width), BF),
            pltpu.VMEM((8, 8, width), BF),
            pltpu.VMEM((8, width), BF),
            pltpu.VMEM((16, 8, width), BF),
            pltpu.VMEM((2, 32, half), BF),
            pltpu.VMEM((2, 4, 2, 2, 32, half), BF),
            pltpu.VMEM((512, 256), F32),
            pltpu.VMEM((512, 256), F32),
            pltpu.VMEM((512, 256), F32),
            pltpu.VMEM((512, 256), BF),
            pltpu.VMEM((4, 2, 128, 640), BF),
            pltpu.VMEM((640, 256), BF),
            pltpu.VMEM((640, 256), BF),
            pltpu.VMEM((4, 4, 128, 256), BF),
            pltpu.VMEM((4, 4, 256, 256), BF),
            pltpu.VMEM((16, 32, quarter), BF),
            pltpu.VMEM((3, 8, 32, quarter), BF),
            pltpu.VMEM((8, 32, quarter), BF),
            pltpu.VMEM((4, 32, quarter), BF),
            pltpu.VMEM((8, 128), jnp.int32),
            pltpu.VMEM((8, 128), jnp.int32),
            dma((3,)),
            dma((7, 8)),
            dma((7,)),
            dma((8,)),
            dma((7,)),
            dma,
            dma((3,)),
            dma((3,)),
            dma((3,)),
            dma((6,)),
            dma((4,)),
            dma((5,)),
            dma((9,)),
            dma((5,)),
            dma((4,)),
            dma,
        ],
        compiler_params=pltpu.CompilerParams(
            collective_id=0, has_side_effects=True, vmem_limit_bytes=58 * 1024 * 1024
        ),
        name="joint_attention",
    )(
        video_length,
        prompt_length,
        prompt_choice,
        video,
        prompt,
        ffn_gain.reshape(1, -1),
        final_gain.reshape(1, -1),
        video_gain.reshape(1, -1),
        ffn_gate,
        ffn_up,
        ffn_down,
        w_text_key,
        w_text_value,
        w_query,
        w_key,
        w_value,
        w_out,
    )


def solution(mesh):
    in_specs = (
        P("vid", "seq", None),
        P("vid"),
        P("vid", "seq", None),
        P(),
        P("vid"),
        P(),
        P(None, "seq"),
        P(None, "seq"),
        P("seq", None),
        P(),
        P(),
        P("vid", "seq"),
        P("vid", "seq"),
        P("vid", "seq"),
        P("vid", "seq"),
        P("vid", "seq"),
        P("seq", "vid"),
    )
    out_specs = P("vid", "seq", None)
    return jax.shard_map(block, mesh=mesh, in_specs=in_specs, out_specs=out_specs, check_vma=False)
```

time: 159 us -> 138 us (0.87)
  Pallas kernels: 156 us -> 135 us
    pallas_call x1, Pallas kernels: 156 us -> 135 us  [block(): pl.pallas_call(kernel, out_shape=jax.ShapeDtypeStruct(video.shape, video....]
where the time goes in v3:
time: 138 us
  Pallas kernels  135 us (98%)
  local copies, waits for them, and re-layouts  1.67 us (1%)
    pallas_call x1, Pallas kernels, block(): pl.pallas_call(kernel, out_shape=jax.ShapeDtypeStruct(video.shape, video....  135 us

profile of v3, /device:TPU:1, one launch (start us, length us, event | category | flops | bytes accessed | tf_op | source)
XLA Modules:
  0.0 137.7 jit_solution(13496842835902504077)
XLA Ops:
  1.3 134.8 %joint_attention.1 = bf16[1,32,4096]{2,1,0:T(8,128)(2,1)} custom-call(s32[1]{0:T(128)S(6)} %copy.19.length_ref, s32[16]{0:T(128)} %prompt_length_ref.1, s32[1]{0:T(128)S(6)} %copy.20.choice_ref, bf16[1,32,4096]{2,1,0:T(8,128)(2,1)} %video_ref.1, bf16[1,8,4096]{2,1,0:T(8,128)(2,1)} %prompt_ref.1, f32[1,4096]{1,0:T(1,128)} %bitcast.3, f32[1,4096]{1,0:T(1,128)} %bitcast.4, ...), custom_call_target="tpu_custom_call" | custom-call | tf_op jit(solution)/shard_map/joint_attention/pallas_call | solution.py:744
  136.1 1.7 %copy.21 = bf16[1,32,4096]{2,1,0:T(8,128)(2,1)} copy(bf16[1,32,4096]{2,1,0:T(8,128)(2,1)} %joint_attention.1) | data formatting | bytes 524288

commit v4 on v3

--- a/solution.py
+++ b/solution.py
@@ -228,21 +228,22 @@
         for h in range(2)
     ]
 
-    @pl.when(diag)
-    def _():
-        for h in range(2):
+    def keep_video(h):
+        @pl.when(diag)
+        def _():
             local(NV.at[h], video_slot(h), video_recv.at[h]).start()
 
-    @pl.when(not_diag)
-    def _():
-        for h in range(2):
+        @pl.when(not_diag)
+        def _():
             own_chip[h].start()
 
     def send_lower():
+        keep_video(0)
         for k in (2, 1, 3):
             video_x(k).start()
 
     def send_upper():
+        keep_video(1)
         for k in (2, 1, 3):
             video_y(k).start()
 
@@ -365,21 +366,24 @@
         FN[pl.ds(pl.multiple_of(i * 16, 16), 16), :] = rms_norm(rows, ffn_gain_ref[...]).astype(BF)
         return carry
 
-    def gate_up(i, carry):
-        at = pl.ds(pl.multiple_of(i * 512, 512), 512)
-        rows = FN[:, at]
-        gate_acc[...] += jnp.dot(rows, gate_ref[at, :], preferred_element_type=F32)
-        up_acc[...] += jnp.dot(rows, up_ref[at, :], preferred_element_type=F32)
-        return carry
-
-    def ffn_up():
+    def ffn_norm():
         pass_chosen.wait_recv()
         lax.fori_loop(0, 8, norm_rows, 0)
-        ffn_copies[0].wait()
-        ffn_copies[1].wait()
-        gate_acc[...] = jnp.zeros_like(gate_acc)
-        up_acc[...] = jnp.zeros_like(up_acc)
-        lax.fori_loop(0, 8, gate_up, 0)
+
+    def ffn_project(weights, acc, copy):
+        copy.wait()
+
+        def step(i, total):
+            at = pl.ds(pl.multiple_of(i * 512, 512), 512)
+            return total + jnp.dot(FN[:, at], weights[at, :], preferred_element_type=F32)
+
+        acc[...] = lax.fori_loop(0, 8, step, jnp.zeros(acc.shape, F32))
+
+    def ffn_gate():
+        ffn_project(gate_ref, gate_acc, ffn_copies[0])
+
+    def ffn_up():
+        ffn_project(up_ref, up_acc, ffn_copies[1])
         hidden[...] = (jax.nn.gelu(gate_acc[...], approximate=True) * up_acc[...]).astype(BF)
 
     def down_proj(i, carry):
@@ -429,18 +433,19 @@
         spread(1, 16, send_text)
 
     def video_rows(j):
-        at = pl.ds(pl.multiple_of((j % 8) * 256, 256), 256)
-        return XG[j // 8, :, :, :, :, at].reshape(512, 256)
+        at = pl.ds(pl.multiple_of((j % 4) * 512, 512), 512)
+        return XG[j // 4, :, :, :, :, at].reshape(512, 512)
 
     def project(w, acc, result):
         sibling_wait(w)
         acc[...] = jnp.zeros_like(acc)
 
         def step(j, carry):
-            acc[...] += jnp.dot(video_rows(j), W[w, j], preferred_element_type=F32)
+            weights = W[w, pl.ds(2 * j, 2)].reshape(512, 256)
+            acc[...] += jnp.dot(video_rows(j), weights, preferred_element_type=F32)
             return carry
 
-        lax.fori_loop(0, 16, step, 0)
+        lax.fori_loop(0, 8, step, 0)
         result[pl.ds(0, 512), :] = acc[...].astype(BF)
 
     def text_key_value(j, carry):
@@ -603,10 +608,10 @@
     swap(K)
     hop(PROMPT, 4)
     pass_prompts.start()
+    swap(V)
     own(Q)
     hop(TK, 1)
     choose_prompt()
-    swap(V)
     hop(TV, 1)
     hop(O, 1)
     hop(Q, 1)
@@ -615,6 +620,8 @@
     pass_chosen_on()
     pass_upper_on()
     pass_lower_on()
+    ffn_norm()
+    ffn_gate()
     ffn_up()
     hop(TK, 2)
     hop(TV, 2)
@@ -636,16 +643,16 @@
     hop(O, 4)
     hop(Q, 4)
     hop(K, 3)
-    hop(V, 3)
-    send_weights()
     video_wait()
     project(Q, q_acc, queries)
+    hop(V, 3)
     hop(K, 4)
+    send_weights()
     project(K, k_acc, keys)
+    hop(V, 4)
     text_projections()
     attention_probs(0, 4)
     pass_weights_on()
-    hop(V, 4)
     project(V, v_acc, values)
     attend_all()
     weights_wait()

time: 138 us -> 131 us (0.949)
  Pallas kernels: 135 us -> 128 us
    pallas_call x1, Pallas kernels: 135 us -> 128 us  [block(): pl.pallas_call(kernel, out_shape=jax.ShapeDtypeStruct(video.shape, video....]
where the time goes in v4:
time: 131 us
  Pallas kernels  128 us (98%)
  local copies, waits for them, and re-layouts  1.67 us (1%)
    pallas_call x1, Pallas kernels, block(): pl.pallas_call(kernel, out_shape=jax.ShapeDtypeStruct(video.shape, video....  128 us

profile of v4, /device:TPU:1, one launch (start us, length us, event | category | flops | bytes accessed | tf_op | source)
XLA Modules:
  0.0 130.6 jit_solution(14099468462790169943)
XLA Ops:
  1.3 127.6 %joint_attention.1 = bf16[1,32,4096]{2,1,0:T(8,128)(2,1)} custom-call(s32[1]{0:T(128)S(6)} %copy.19.length_ref, s32[16]{0:T(128)} %prompt_length_ref.1, s32[1]{0:T(128)S(6)} %copy.20.choice_ref, bf16[1,32,4096]{2,1,0:T(8,128)(2,1)} %video_ref.1, bf16[1,8,4096]{2,1,0:T(8,128)(2,1)} %prompt_ref.1, f32[1,4096]{1,0:T(1,128)} %bitcast.3, f32[1,4096]{1,0:T(1,128)} %bitcast.4, ...), custom_call_target="tpu_custom_call" | custom-call | tf_op jit(solution)/shard_map/joint_attention/pallas_call | solution.py:751
  128.9 1.7 %copy.21 = bf16[1,32,4096]{2,1,0:T(8,128)(2,1)} copy(bf16[1,32,4096]{2,1,0:T(8,128)(2,1)} %joint_attention.1) | data formatting | bytes 524288

commit v5 on v4

--- a/solution.py
+++ b/solution.py
@@ -85,8 +85,6 @@
     video_send,
     out_recv,
     out_send,
-    weight_sem,
-    weight_recv,
 ):
     vid, seq = lax.axis_index("vid"), lax.axis_index("seq")
     yh, z = vid // 8, vid % 8
@@ -150,7 +148,7 @@
     sources = [w_text_key, w_text_value, w_query, w_key, w_value, w_out, prompt_ref.at[0]]
 
     def slot(w, block):
-        return PB.at[block] if w == PROMPT else W.at[w, block]
+        return PB.at[block] if w == PROMPT else OX.at[block] if w == O else W.at[w, block]
 
     def swap_copy(w):
         return remote(sources[w], slot(w, yh * 8 + z), swap_send.at[w], ring_recv.at[w, z], taker)
@@ -159,8 +157,23 @@
     swap_copy(PROMPT).start()
     info_copy.start()
 
+    def swap_half(half):
+        taker_y = (yl + 1 + 2 * c) % 4
+        device = ((taker_y // 2) * 8 + z, (2 * yh + half) * 4 + (taker_y % 2) * 2 + x // 2)
+        return remote(
+            w_out.at[:, pl.ds(half * 128, 128)],
+            OX.at[(x // 2) * 8 + z, x % 2],
+            swap_send.at[O],
+            ring_recv.at[O, z],
+            device,
+        )
+
     def swap(w):
-        swap_copy(w).start()
+        if w == O:
+            swap_half(0).start()
+            swap_half(1).start()
+        else:
+            swap_copy(w).start()
 
     def ring_wait(w, zz):
         ref = slot(w, c * 8 + zz)
@@ -171,7 +184,7 @@
         remote(ref, ref, ring_send.at[w], ring_recv.at[w, zz], device).start()
 
     def to_sibling(w, zz):
-        if w in (O, PROMPT):
+        if w == PROMPT:
             return
         ref = slot(w, c * 8 + zz)
         remote(ref, ref, ring_send.at[w], sib_recv.at[w], sibling).start()
@@ -200,7 +213,7 @@
             to_sibling(w, from_right)
 
     def sibling_wait(w):
-        ref = W.at[w, pl.ds(0, 8)]
+        ref = OX.at[pl.ds(0, 8)] if w == O else W.at[w, pl.ds(0, 8)]
         local(ref, ref, sib_recv.at[w]).wait()
 
     not_diag = jnp.logical_not(diag)
@@ -464,38 +477,6 @@
         text_key, text_value = lax.fori_loop(0, 16, text_key_value, (zero, zero))
         keys[pl.ds(512, 128), :] = text_key.astype(BF)
         values[pl.ds(512, 128), :] = text_value.astype(BF)
-
-    mine = x // 2 == c
-
-    def weight_copy(i):
-        xk = 2 * c + i
-        return remote(
-            W.at[O, pl.ds(pl.multiple_of(xk * 4, 4), 4)], OX.at[x], weight_sem.at[i], weight_recv, at_core(xk, y, c)
-        )
-
-    def send_weights():
-        for i in range(2):
-
-            @pl.when(x != 2 * c + i)
-            def _():
-                weight_copy(i).start()
-
-            @pl.when(x == 2 * c + i)
-            def _():
-                local(W.at[O, pl.ds(pl.multiple_of(x * 4, 4), 4)], OX.at[x], weight_recv).start()
-
-    pass_weights = remote(OX, OX, weight_sem.at[2], weight_sem.at[3], sibling)
-
-    def pass_weights_on():
-        @pl.when(mine)
-        def _():
-            local(OX, OX, weight_recv).wait()
-            pass_weights.start()
-
-    def weights_wait():
-        @pl.when(jnp.logical_not(mine))
-        def _():
-            pass_weights.wait_recv()
 
     def attended_x(part, xk):
         ref = AX.at[x, part]
@@ -557,10 +538,14 @@
         part = (x + 1 + i) % 4
         ref = AX.at[pl.ds(0, 3), 0]
         local(ref, ref, out_recv.at[part]).wait()
+        rows = [jnp.concatenate([AX[2 * j, part], AX[2 * j + 1, part]], axis=1) for j in range(2)]
         for m in range(4):
-            total = jnp.dot(AX[0, part], OX[0, m], preferred_element_type=F32)
-            for j in range(1, 4):
-                total = total + jnp.dot(AX[j, part], OX[j, m], preferred_element_type=F32)
+            total = jnp.zeros((128, 256), F32)
+            for j in range(2):
+                weights = jnp.concatenate(
+                    [OX[j * 8 + 2 * m + i].reshape(512, 128) for i in range(2)], axis=1
+                )
+                total = total + jnp.dot(rows[j], weights, preferred_element_type=F32)
             SB[pl.ds(part * 4, 4), :, pl.ds(m * 256, 256)] = total.reshape(4, 32, 256).astype(BF)
         for k in range(2):
 
@@ -594,28 +579,28 @@
 
     send_lower()
     swap(TK)
-    send_upper()
     own(PROMPT)
     swap(TV)
+    hop(PROMPT, 1)
+    send_upper()
+    swap(Q)
     own(TK)
-    hop(PROMPT, 1)
+    hop(PROMPT, 2)
+    own(TV)
+    swap(K)
+    hop(PROMPT, 3)
+    own(Q)
     swap(O)
-    own(TV)
-    hop(PROMPT, 2)
-    swap(Q)
-    hop(PROMPT, 3)
-    own(O)
-    swap(K)
     hop(PROMPT, 4)
     pass_prompts.start()
     swap(V)
-    own(Q)
+    own(K)
     hop(TK, 1)
     choose_prompt()
     hop(TV, 1)
-    hop(O, 1)
     hop(Q, 1)
-    own(K)
+    hop(K, 1)
+    own(O)
     own(V)
     pass_chosen_on()
     pass_upper_on()
@@ -625,37 +610,35 @@
     ffn_up()
     hop(TK, 2)
     hop(TV, 2)
-    hop(O, 2)
     hop(Q, 2)
-    hop(K, 1)
+    hop(K, 2)
+    hop(O, 1)
     ffn_down()
     hop(V, 1)
     hop(TK, 3)
     ffn_sums()
     hop(TV, 3)
-    hop(O, 3)
     hop(Q, 3)
-    hop(K, 2)
+    hop(K, 3)
+    hop(O, 2)
     hop(V, 2)
     text_rows()
     hop(TK, 4)
     hop(TV, 4)
-    hop(O, 4)
     hop(Q, 4)
-    hop(K, 3)
+    hop(K, 4)
     video_wait()
     project(Q, q_acc, queries)
+    hop(O, 3)
     hop(V, 3)
-    hop(K, 4)
-    send_weights()
     project(K, k_acc, keys)
     hop(V, 4)
     text_projections()
     attention_probs(0, 4)
-    pass_weights_on()
     project(V, v_acc, values)
+    hop(O, 4)
     attend_all()
-    weights_wait()
+    sibling_wait(O)
     lax.fori_loop(0, 4, project_part, 0)
 
     @pl.when(diag)
@@ -667,12 +650,15 @@
     row_live = row_position < length_ref[0]
 
     for j in range(4):
-        at = pl.ds(j * 1024, 1024)
-        updated = video_ref[0, :, at].astype(F32) + jnp.where(row_live, RR[j].astype(F32), 0.0)
-        out_ref[0, :, at] = updated.astype(BF)
-
-    for w in range(7):
+        for i in range(8):
+            at = pl.ds((j // 2) * 2048 + i * 256 + (j % 2) * 128, 128)
+            total = RR[j, :, pl.ds(i * 128, 128)].astype(F32)
+            updated = video_ref[0, :, at].astype(F32) + jnp.where(row_live, total, 0.0)
+            out_ref[0, :, at] = updated.astype(BF)
+
+    for w in (TK, TV, Q, K, V, PROMPT):
         swap_copy(w).wait_send()
+    local(OX.at[0], OX.at[0], swap_send.at[O]).wait()
     info_copy.wait_send()
 
     @pl.when(jnp.logical_not(diag))
@@ -683,7 +669,7 @@
 
     pass_prompts.wait_send()
     for w in range(7):
-        ref = PB.at[pl.ds(0, 7)] if w == PROMPT else W.at[w, pl.ds(0, 7 if w == O else 15)]
+        ref = slot(w, pl.ds(0, 7 if w == PROMPT else 15))
         local(ref, ref, ring_send.at[w]).wait()
     @pl.when(jnp.logical_not(chosen_here))
     def _():
@@ -703,18 +689,10 @@
     local(ref, ref, out_send.at[0]).wait()
     for k in range(2):
 
-        @pl.when(x != 2 * c + k)
-        def _():
-            weight_copy(k).wait_send()
-
         @pl.when(y != c * 2 + k)
         def _():
             ref = SB.at[pl.ds(0, 8)]
             local(ref, ref, out_send.at[1 + k]).wait()
-
-    @pl.when(mine)
-    def _():
-        pass_weights.wait_send()
 
     @pl.when(diag)
     def _():
@@ -754,7 +732,7 @@
         in_specs=[smem] * 3 + [vmem] * 5 + [hbm] * 9,
         out_specs=vmem,
         scratch_shapes=[
-            pltpu.VMEM((6, 16, 256, 256), BF),
+            pltpu.VMEM((5, 16, 256, 256), BF),
             pltpu.VMEM((16, 8, width), BF),
             pltpu.VMEM((8, width), BF),
             pltpu.VMEM((16, 8, width), BF),
@@ -781,7 +759,7 @@
             pltpu.VMEM((640, 256), BF),
             pltpu.VMEM((640, 256), BF),
             pltpu.VMEM((4, 4, 128, 256), BF),
-            pltpu.VMEM((4, 4, 256, 256), BF),
+            pltpu.VMEM((16, 2, 256, 128), BF),
             pltpu.VMEM((16, 32, quarter), BF),
             pltpu.VMEM((3, 8, 32, quarter), BF),
             pltpu.VMEM((8, 32, quarter), BF),
@@ -802,8 +780,6 @@
             dma((5,)),
             dma((9,)),
             dma((5,)),
-            dma((4,)),
-            dma,
         ],
         compiler_params=pltpu.CompilerParams(
             collective_id=0, has_side_effects=True, vmem_limit_bytes=58 * 1024 * 1024

time: 131 us -> 123 us (0.939)
  Pallas kernels: 128 us -> 119 us
    pallas_call x1, Pallas kernels: 128 us -> 119 us  [block(): pl.pallas_call(kernel, out_shape=jax.ShapeDtypeStruct(video.shape, video....]
where the time goes in v5:
time: 123 us; the launch traced here: 122 us
  Pallas kernels  119 us (97%)
  local copies, waits for them, and re-layouts  1.67 us (1%)
  between operations  1.3 us (1%)
    pallas_call x1, Pallas kernels, block(): pl.pallas_call(kernel, out_shape=jax.ShapeDtypeStruct(video.shape, video....  119 us

profile of v5, /device:TPU:1, one launch (start us, length us, event | category | flops | bytes accessed | tf_op | source)
XLA Modules:
  0.0 122.2 jit_solution(6772440903928347137)
XLA Ops:
  1.3 119.2 %joint_attention.1 = bf16[1,32,4096]{2,1,0:T(8,128)(2,1)} custom-call(s32[1]{0:T(128)S(6)} %copy.19.length_ref, s32[16]{0:T(128)} %prompt_length_ref.1, s32[1]{0:T(128)S(6)} %copy.20.choice_ref, bf16[1,32,4096]{2,1,0:T(8,128)(2,1)} %video_ref.1, bf16[1,8,4096]{2,1,0:T(8,128)(2,1)} %prompt_ref.1, f32[1,4096]{1,0:T(1,128)} %bitcast.3, f32[1,4096]{1,0:T(1,128)} %bitcast.4, ...), custom_call_target="tpu_custom_call" | custom-call | tf_op jit(solution)/shard_map/joint_attention/pallas_call | solution.py:729
  120.5 1.7 %copy.21 = bf16[1,32,4096]{2,1,0:T(8,128)(2,1)} copy(bf16[1,32,4096]{2,1,0:T(8,128)(2,1)} %joint_attention.1) | data formatting | bytes 524288

commit v6 on v5

--- a/solution.py
+++ b/solution.py
@@ -586,13 +586,13 @@
     swap(Q)
     own(TK)
     hop(PROMPT, 2)
-    own(TV)
     swap(K)
     hop(PROMPT, 3)
-    own(Q)
+    own(TV)
     swap(O)
     hop(PROMPT, 4)
     pass_prompts.start()
+    own(Q)
     swap(V)
     own(K)
     hop(TK, 1)

time: 123 us -> 123 us (level)
  no operation moved by 1% of the time
where the time goes in v6:
time: 123 us
  Pallas kernels  120 us (98%)
  local copies, waits for them, and re-layouts  1.67 us (1%)
  between operations  1.3 us (1%)
    pallas_call x1, Pallas kernels, block(): pl.pallas_call(kernel, out_shape=jax.ShapeDtypeStruct(video.shape, video....  120 us

profile of v6, /device:TPU:1, one launch (start us, length us, event | category | flops | bytes accessed | tf_op | source)
XLA Modules:
  0.0 122.9 jit_solution(8517690549275632575)
XLA Ops:
  1.3 119.9 %joint_attention.1 = bf16[1,32,4096]{2,1,0:T(8,128)(2,1)} custom-call(s32[1]{0:T(128)S(6)} %copy.19.length_ref, s32[16]{0:T(128)} %prompt_length_ref.1, s32[1]{0:T(128)S(6)} %copy.20.choice_ref, bf16[1,32,4096]{2,1,0:T(8,128)(2,1)} %video_ref.1, bf16[1,8,4096]{2,1,0:T(8,128)(2,1)} %prompt_ref.1, f32[1,4096]{1,0:T(1,128)} %bitcast.3, f32[1,4096]{1,0:T(1,128)} %bitcast.4, ...), custom_call_target="tpu_custom_call" | custom-call | tf_op jit(solution)/shard_map/joint_attention/pallas_call | solution.py:729
  121.2 1.7 %copy.21 = bf16[1,32,4096]{2,1,0:T(8,128)(2,1)} copy(bf16[1,32,4096]{2,1,0:T(8,128)(2,1)} %joint_attention.1) | data formatting | bytes 524288
